TPU v7x, 32 devices: a whole 2x2x4 slice. The times are simulated.
32 devices in a mesh: rep: 4 (over y, core), fsdp: 8 (over z, x).
Axes of the slice: x: 2, y: 2, z: 4, core: 2. Of those that a mesh axis runs over, the one named last changes fastest.
Arguments:
- tokens: bfloat16 [8192, 1024], P(('rep', 'fsdp')), may hold values from -6 to 6
- segment_ids: int32 [8192], P(('rep', 'fsdp')), may hold values from 0 to 7, as said below
- positions: int32 [8192], P(('rep', 'fsdp')), may hold values from 0 to 1023, as said below
- attn_gain: bfloat16 [2, 1024], P(None, 'fsdp'), may hold values from 0.099609375 to 1.8984375
- w_qkv: bfloat16 [2, 1024, 3072], P(None, 'fsdp'), may hold values from -0.1875 to 0.1875
- w_out: bfloat16 [2, 1024, 1024], P(None, 'fsdp'), may hold values from -2 to 2
- mlp_gain: bfloat16 [2, 1024], P(None, 'fsdp'), may hold values from 0.099609375 to 1.8984375
- w_in: bfloat16 [2, 1024, 5248], P(None, 'fsdp'), may hold values from -0.1875 to 0.1875
- w_down: bfloat16 [2, 2624, 1024], P(None, 'fsdp'), may hold values from -0.125 to 0.125
- cotangent: bfloat16 [8192, 1024], P(('rep', 'fsdp')), may hold values from -6 to 6
Outputs:
- block_output: bfloat16 [8192, 1024], P(('rep', 'fsdp'))
- grad_tokens: float32 [8192, 1024], P(('rep', 'fsdp'))
- grad_attn_gain: float32 [2, 1024], P(None, 'fsdp')
- grad_w_qkv: float32 [2, 1024, 3072], P(None, 'fsdp')
- grad_w_out: float32 [2, 1024, 1024], P(None, 'fsdp')
- grad_mlp_gain: float32 [2, 1024], P(None, 'fsdp')
- grad_w_in: float32 [2, 1024, 5248], P(None, 'fsdp')
- grad_w_down: float32 [2, 2624, 1024], P(None, 'fsdp')
Inputs may be any that keep to these rules, and one draw needn't show every extreme that they name: `segment_ids`: each index of rep holds two sequences of 1024 tokens each, and no value is shared by two sequences. Every device of a group holds a block of the group's first sequence followed by a block of its second; each block has 64 to 192 tokens. Within one sequence each position occurs once; positions start at 0 and rise by one along a sequence's tokens, within a device and from each device to the next along fsdp.
All inputs are finite; a program needn't handle non-finite values.
Results may differ from a plain program's by a relative error of at most 0.023.
Values may be sent and summed in bfloat16 or wider, within the bound.
A program may use at most 320 MiB of HBM per device.

v0:
```python
import jax
import jax.numpy as jnp
from jax import lax
from jax.sharding import PartitionSpec as P

D = 1024
HEADS = 16
HEAD_DIM = 64
FF = 2624
HALF_WINDOW = 64
LAYERS = 2


LOCAL_THETA = 10000.0
GLOBAL_THETA = 160000.0
MASKED_SCORE = -1e30
NORM_EPSILON = 1e-05


def shortened(x):
    return jax.tree.map(lambda a: a.astype(jnp.bfloat16) if a.dtype == jnp.float32 else a, x)


def shifted(value, axis, steps):
    count = lax.axis_size(axis)
    first, last = (max(0, -steps), min(count, count - steps))
    return lax.ppermute(value, axis, [(source, source + steps) for source in range(first, last)])


def layer_norm(values, gain_row):
    center = values - jnp.mean(values, axis=-1, keepdims=True)
    spread = jnp.mean(center * center, axis=-1, keepdims=True)
    return center * lax.rsqrt(spread + NORM_EPSILON) * gain_row


def rotate(matrix, places, base_theta):
    row_count = matrix.shape[0]
    shaped = matrix.reshape(row_count, HEADS, HEAD_DIM)
    half_dim = HEAD_DIM // 2
    frequency = jnp.power(base_theta, -2.0 * jnp.arange(half_dim, dtype=jnp.float32) / HEAD_DIM)
    angles = places.astype(jnp.float32)[:, None] * frequency[None, :]
    cosine = jnp.cos(angles)[:, None, :]
    sine_part = jnp.sin(angles)[:, None, :]
    first_half = shaped[..., :half_dim]
    second_half = shaped[..., half_dim:]
    turned = jnp.concatenate(
        [
            first_half * cosine - second_half * sine_part,
            second_half * cosine + first_half * sine_part,
        ],
        axis=-1,
    )
    return turned.reshape(row_count, HEADS * HEAD_DIM)


def rotate_back(gradient, places, base_theta):
    turned, pull_back = jax.vjp(lambda rotated_in: rotate(rotated_in, places, base_theta), gradient)
    return pull_back(gradient)[0]


def gelu_gate(raised):
    return jax.nn.gelu(raised[:, :FF], approximate=False) * raised[:, FF:]


def contract_rows(left, right):
    return lax.dot_general(
        left, right, (((0,), (0,)), ((), ())), preferred_element_type=jnp.float32
    )


def contract_cols(left, right):
    return lax.dot_general(
        left, right, (((1,), (1,)), ((), ())), preferred_element_type=jnp.float32
    )


def head_block(matrix, group_index, head_width):
    columns = lax.dynamic_slice_in_dim(
        matrix, group_index * head_width * HEAD_DIM, head_width * HEAD_DIM, 1
    )
    return columns.reshape(matrix.shape[0], head_width, HEAD_DIM)


def merge_heads(stacked):
    return jnp.transpose(stacked, (1, 0, 2)).reshape(stacked.shape[1], HEADS * HEAD_DIM)


def neighbour_window(own, fetch):
    pieces = [fetch(own, -2), fetch(own, -1), own, fetch(own, 1), fetch(own, 2)]
    return tuple(
        (jnp.concatenate([piece[member] for piece in pieces], axis=0) for member in range(len(own)))
    )


def attend_forward(queries, key_rows, value_rows, allowed):
    head_width = min(4, HEADS)
    score_scale = HEAD_DIM ** (-0.5)

    def one_group(group_index):
        query_block = head_block(queries, group_index, head_width)
        key_block = head_block(key_rows, group_index, head_width)
        value_block = head_block(value_rows, group_index, head_width)
        scores = (
            jnp.einsum("qhd,khd->hqk", query_block, key_block, preferred_element_type=jnp.float32)
            * score_scale
        )
        scores = jnp.where(allowed[None], scores, MASKED_SCORE)
        highest = jnp.max(scores, axis=-1, keepdims=True)
        raised = jnp.exp(scores - highest)
        totals = jnp.sum(raised, axis=-1, keepdims=True)
        soft_weights = (raised / totals).astype(jnp.bfloat16)
        outputs = jnp.einsum(
            "hqk,khd->qhd", soft_weights, value_block, preferred_element_type=jnp.float32
        )
        return (
            outputs.reshape(outputs.shape[0], head_width * HEAD_DIM),
            (highest + jnp.log(totals))[..., 0],
        )

    outputs, log_sums = lax.map(one_group, jnp.arange(HEADS // head_width, dtype=jnp.int32))
    return (merge_heads(outputs), log_sums)


def attend_backward(queries, key_rows, value_rows, grad_mixed, log_sums, allowed):
    head_width = min(4, HEADS)
    score_scale = HEAD_DIM ** (-0.5)

    def one_group(carried):
        group_index, group_sums = carried
        query_block = head_block(queries, group_index, head_width)
        key_block = head_block(key_rows, group_index, head_width)
        value_block = head_block(value_rows, group_index, head_width)
        grad_block = head_block(grad_mixed, group_index, head_width)
        scores = (
            jnp.einsum("qhd,khd->hqk", query_block, key_block, preferred_element_type=jnp.float32)
            * score_scale
        )
        scores = jnp.where(allowed[None], scores, MASKED_SCORE)
        soft_weights = jnp.exp(scores - group_sums[..., None])
        grad_soft = jnp.einsum(
            "qhd,khd->hqk", grad_block, value_block, preferred_element_type=jnp.float32
        )
        inner_sum = jnp.sum(soft_weights * grad_soft, axis=-1, keepdims=True)
        grad_scores = (soft_weights * (grad_soft - inner_sum)).astype(jnp.bfloat16)
        grad_query = (
            jnp.einsum("hqk,khd->qhd", grad_scores, key_block, preferred_element_type=jnp.float32)
            * score_scale
        )
        grad_query = grad_query.reshape(grad_query.shape[0], head_width * HEAD_DIM)
        grad_key = (
            jnp.einsum("hqk,qhd->khd", grad_scores, query_block, preferred_element_type=jnp.float32)
            * score_scale
        )
        grad_value = jnp.einsum(
            "hqk,qhd->khd",
            soft_weights.astype(jnp.bfloat16),
            grad_block,
            preferred_element_type=jnp.float32,
        )
        return (
            grad_query,
            grad_key.reshape(grad_key.shape[0], head_width * HEAD_DIM),
            grad_value.reshape(grad_value.shape[0], head_width * HEAD_DIM),
            inner_sum[..., 0],
        )

    results = lax.map(one_group, (jnp.arange(HEADS // head_width, dtype=jnp.int32), log_sums))
    return (merge_heads(results[0]), merge_heads(results[1]), merge_heads(results[2]), results[3])


def on_device(
    tokens, segment_ids, positions, attn_gain, w_qkv, w_out, mlp_gain, w_in, w_down, cotangent
):
    row_count = tokens.shape[0]
    hidden = tokens.astype(jnp.float32)
    memory = []

    def fetch_window(member, offset):
        return jax.tree.map(
            lambda part, own: part.astype(own.dtype),
            shifted(shortened(member), "fsdp", -offset),
            member,
        )

    def fetch_window_again(member, offset):
        return jax.tree.map(
            lambda part, own: part.astype(own.dtype),
            shifted(shortened(member), "fsdp", -offset),
            member,
        )

    for layer_index in range(LAYERS):
        base_theta = LOCAL_THETA if layer_index == 0 else GLOBAL_THETA
        weights = (
            lax.all_gather(attn_gain[layer_index], "fsdp", axis=0, tiled=True),
            lax.all_gather(w_qkv[layer_index], "fsdp", axis=0, tiled=True),
            lax.all_gather(w_out[layer_index], "fsdp", axis=0, tiled=True),
            lax.all_gather(mlp_gain[layer_index], "fsdp", axis=0, tiled=True),
            lax.all_gather(w_in[layer_index], "fsdp", axis=0, tiled=True),
            lax.all_gather(w_down[layer_index], "fsdp", axis=0, tiled=True),
        )
        gain_attn, mat_qkv, mat_out, gain_mlp, mat_in, mat_down = weights
        normed = layer_norm(hidden, gain_attn.astype(jnp.float32)).astype(jnp.bfloat16)
        projected = jnp.dot(normed, mat_qkv, preferred_element_type=jnp.float32)
        queries = rotate(projected[:, :D], positions, base_theta).astype(jnp.bfloat16)
        key_local = rotate(projected[:, D : 2 * D], positions, base_theta).astype(jnp.bfloat16)
        value_local = projected[:, 2 * D :].astype(jnp.bfloat16)
        if layer_index == 0:
            key_rows, value_rows, key_segments, key_places = neighbour_window(
                (key_local, value_local, segment_ids + 1, positions), fetch_window
            )
            allowed = (segment_ids[:, None] + 1 == key_segments[None, :]) & (
                jnp.abs(positions[:, None] - key_places[None, :]) <= HALF_WINDOW
            )
        else:
            key_rows, value_rows, key_segments, key_places = (
                lax.all_gather(key_local, "fsdp", axis=0, tiled=True),
                lax.all_gather(value_local, "fsdp", axis=0, tiled=True),
                lax.all_gather(segment_ids, "fsdp", axis=0, tiled=True),
                lax.all_gather(positions, "fsdp", axis=0, tiled=True),
            )
            allowed = segment_ids[:, None] == key_segments[None, :]
        attended, log_sums = attend_forward(queries, key_rows, value_rows, allowed)
        attended = attended.astype(jnp.bfloat16)
        middle = hidden + jnp.dot(attended, mat_out, preferred_element_type=jnp.float32)
        normed_mlp = layer_norm(middle, gain_mlp.astype(jnp.float32)).astype(jnp.bfloat16)
        raised = jnp.dot(normed_mlp, mat_in, preferred_element_type=jnp.float32)
        gated_hidden = gelu_gate(raised).astype(jnp.bfloat16)
        output = middle + jnp.dot(gated_hidden, mat_down, preferred_element_type=jnp.float32)
        kept_copies = (None, None, None)
        memory.append(
            (
                hidden,
                normed,
                queries,
                key_local,
                value_local,
                key_segments,
                allowed,
                attended,
                log_sums,
                middle,
                normed_mlp,
                raised,
                gated_hidden,
                kept_copies,
            )
        )
        hidden = output
    grad_hidden = cotangent.astype(jnp.float32)
    owned = [None, None]
    for layer_index in range(LAYERS - 1, -1, -1):
        base_theta = LOCAL_THETA if layer_index == 0 else GLOBAL_THETA
        (
            layer_input,
            normed,
            queries,
            key_local,
            value_local,
            key_segments,
            allowed,
            attended,
            log_sums,
            middle,
            normed_mlp,
            raised,
            gated_hidden,
            kept_copies,
        ) = memory[layer_index]
        weights = (
            lax.all_gather(attn_gain[layer_index], "fsdp", axis=0, tiled=True),
            lax.all_gather(w_qkv[layer_index], "fsdp", axis=0, tiled=True),
            lax.all_gather(w_out[layer_index], "fsdp", axis=0, tiled=True),
            lax.all_gather(mlp_gain[layer_index], "fsdp", axis=0, tiled=True),
            lax.all_gather(w_in[layer_index], "fsdp", axis=0, tiled=True),
            lax.all_gather(w_down[layer_index], "fsdp", axis=0, tiled=True),
        )
        if layer_index == 0:
            key_rows, value_rows = neighbour_window((key_local, value_local), fetch_window_again)
        else:
            key_rows, value_rows = (
                lax.all_gather(key_local, "fsdp", axis=0, tiled=True),
                lax.all_gather(value_local, "fsdp", axis=0, tiled=True),
            )
        gain_attn, mat_qkv, mat_out, gain_mlp, mat_in, mat_down = weights
        grad_branch = grad_hidden.astype(jnp.bfloat16)
        grad_gated = contract_cols(grad_branch, mat_down)
        unused, pull_gate = jax.vjp(gelu_gate, raised)
        grad_raised = pull_gate(grad_gated)[0].astype(jnp.bfloat16)
        grad_normed_mlp = contract_cols(grad_raised, mat_in)
        unused, pull_norm = jax.vjp(layer_norm, middle, gain_mlp.astype(jnp.float32))
        grad_middle_part, grad_gain_mlp = pull_norm(grad_normed_mlp)
        grad_middle = grad_hidden + grad_middle_part
        grad_attn_in = grad_middle.astype(jnp.bfloat16)
        grad_mixed = contract_cols(grad_attn_in, mat_out).astype(jnp.bfloat16)
        if layer_index == 0:
            grad_queries, grad_keys, grad_values, inner = attend_backward(
                queries, key_rows, value_rows, grad_mixed, log_sums, allowed
            )
            window_grads = jnp.concatenate([grad_keys, grad_values], axis=1).reshape(
                5, row_count, 2 * D
            )
            summed = window_grads[2]
            for place, offset in ((0, -2), (1, -1), (3, 1), (4, 2)):
                piece = window_grads[place]
                summed = summed + shifted(piece.astype(jnp.bfloat16), "fsdp", offset).astype(
                    piece.dtype
                )
        else:
            grad_queries, grad_keys, grad_values, inner = attend_backward(
                queries, key_rows, value_rows, grad_mixed, log_sums, allowed
            )
            summed = lax.psum_scatter(
                jnp.concatenate([grad_keys, grad_values], axis=1).astype(jnp.bfloat16),
                "fsdp",
                scatter_dimension=0,
                tiled=True,
            ).astype(jnp.float32)
        grad_projected = jnp.concatenate(
            [
                rotate_back(grad_queries, positions, base_theta),
                rotate_back(summed[:, :D], positions, base_theta),
                summed[:, D:],
            ],
            axis=1,
        ).astype(jnp.bfloat16)
        grad_normed = contract_cols(grad_projected, mat_qkv)
        unused, pull_first = jax.vjp(layer_norm, layer_input, gain_attn.astype(jnp.float32))
        grad_hidden_part, grad_gain_attn = pull_first(grad_normed)
        grad_hidden = grad_middle + grad_hidden_part
        grad_w_qkv = contract_rows(normed, grad_projected)
        grad_w_out = contract_rows(attended, grad_attn_in)
        grad_w_in = contract_rows(normed_mlp, grad_raised)
        grad_w_down = contract_rows(gated_hidden, grad_branch)
        shares = (
            lax.psum_scatter(
                grad_gain_attn.astype(jnp.bfloat16), "fsdp", scatter_dimension=0, tiled=True
            ).astype(jnp.float32),
            lax.psum_scatter(
                grad_w_qkv.astype(jnp.bfloat16), "fsdp", scatter_dimension=0, tiled=True
            ).astype(jnp.float32),
            lax.psum_scatter(
                grad_w_out.astype(jnp.bfloat16), "fsdp", scatter_dimension=0, tiled=True
            ).astype(jnp.float32),
            lax.psum_scatter(
                grad_gain_mlp.astype(jnp.bfloat16), "fsdp", scatter_dimension=0, tiled=True
            ).astype(jnp.float32),
            lax.psum_scatter(
                grad_w_in.astype(jnp.bfloat16), "fsdp", scatter_dimension=0, tiled=True
            ).astype(jnp.float32),
            lax.psum_scatter(
                grad_w_down.astype(jnp.bfloat16), "fsdp", scatter_dimension=0, tiled=True
            ).astype(jnp.float32),
        )
        shares = (
            lax.psum(shares[0].astype(jnp.bfloat16), "rep").astype(jnp.float32),
            lax.psum(shares[1].astype(jnp.bfloat16), "rep").astype(jnp.float32),
            lax.psum(shares[2].astype(jnp.bfloat16), "rep").astype(jnp.float32),
            lax.psum(shares[3].astype(jnp.bfloat16), "rep").astype(jnp.float32),
            lax.psum(shares[4].astype(jnp.bfloat16), "rep").astype(jnp.float32),
            lax.psum(shares[5].astype(jnp.bfloat16), "rep").astype(jnp.float32),
        )
        owned[layer_index] = tuple(shares)
    results = tuple((jnp.stack([owned[0][member], owned[1][member]]) for member in range(6)))
    return (hidden.astype(jnp.bfloat16), grad_hidden) + results


def solution(mesh):
    return jax.shard_map(
        on_device,
        mesh=mesh,
        in_specs=(
            P(("rep", "fsdp"), None),
            P(("rep", "fsdp")),
            P(("rep", "fsdp")),
            P(None, "fsdp"),
            P(None, "fsdp", None),
            P(None, "fsdp", None),
            P(None, "fsdp"),
            P(None, "fsdp", None),
            P(None, "fsdp", None),
            P(("rep", "fsdp"), None),
        ),
        out_specs=(
            P(("rep", "fsdp"), None),
            P(("rep", "fsdp"), None),
            P(None, "fsdp"),
            P(None, "fsdp", None),
            P(None, "fsdp", None),
            P(None, "fsdp"),
            P(None, "fsdp", None),
            P(None, "fsdp", None),
        ),
        check_vma=False,
    )
```

profile of v0, /device:TPU:0, one launch (start us, length us, event | category | flops | bytes accessed | tf_op | source)
XLA Modules:
  0.0 2404.8 jit_solution(10979310941035926717)
XLA Ops:
  33.1 19.1 all-gather
  53.2 16.5 all-gather.3
  69.7 18.4 all-gather.6
  97.8 15.0 all-gather.28.cloned.1.call-done
  177.9 17.8 collective-permute-done.15
  198.3 31.3 %while.64 = (s32[]{:T(128)}, bf16[4,256,256]{1,2,0:T(8,128)(2,1)}, f32[4,4,256]{2,1,0:T(4,128)S(1)}, s32[4]{0:T(128)S(1)}, bf16[1280,1024]{0,1:T(8,128)(2,1)S(1)...) while((s32[]{:T(128)}, bf16[4,256,256]{1,2,0:T(8,128)(2,1)}, ...), condition=%wide.region_5.6_spmd.clone, body=%wide.region_2.5_spmd.clone.sunk | while | flops 347667456 | bytes 21147872 | solution.py:120
  234.5 104.7 %all-gather.32.cloned.1.call-done = bf16[1,1024,5248]{2,1,0:T(8,128)(2,1)} async-done(((bf16[1,128,5248]{2,1,0:T(8,128)(2,1)}), bf16[1,1024,5248]{2,1,0:T(8,128)(2,1)}) %all-gather.32.cloned.1.call-update) | async-done | bytes 10747920 | tf_op jit(solution)/shard_map/all_gather | solution.py:199
  355.1 72.2 %all-gather.34.cloned.1.call-done = bf16[1,2624,1024]{2,1,0:T(8,128)(2,1)} async-done(((bf16[1,328,1024]{2,1,0:T(8,128)(2,1)}), bf16[1,2624,1024]{2,1,0:T(8,128)(2,1)}) %all-gather.34.cloned.1.call-update) | async-done | bytes 5373968 | tf_op jit(solution)/shard_map/all_gather | solution.py:200
  432.5 94.6 %all-gather.36.cloned.1.call-done = bf16[1,1024,3072]{2,1,0:T(8,128)(2,1)} async-done(((bf16[1,128,3072]{2,1,0:T(8,128)(2,1)}), bf16[1,1024,3072]{2,1,0:T(8,128)(2,1)}) %all-gather.36.cloned.1.call-update) | async-done | bytes 6291472 | tf_op jit(solution)/shard_map/all_gather | solution.py:196
  543.2 17.8 all-gather.12
  561.0 17.3 all-gather.9
  578.5 27.8 %all-gather.24.cloned.1.call-done = bf16[2048,1024]{1,0:T(8,128)(2,1)} async-done(((bf16[256,1024]{1,0:T(8,128)(2,1)}), bf16[2048,1024]{1,0:T(8,128)(2,1)}) %all-gather.24.cloned.1.call-update) | async-done | bytes 4194320 | tf_op jit(solution)/shard_map/all_gather | solution.py:218
  612.8 69.4 %all-gather.26.cloned.1.call-done = bf16[2048,1024]{0,1:T(8,128)(2,1)} async-done(((bf16[256,1024]{0,1:T(8,128)(2,1)}), bf16[2048,1024]{0,1:T(8,128)(2,1)}) %all-gather.26.cloned.1.call-update) | async-done | bytes 4194320 | tf_op jit(solution)/shard_map/all_gather | solution.py:217
  682.2 40.8 %while.65 = (s32[]{:T(128)}, bf16[4,256,256]{1,2,0:T(8,128)(2,1)S(1)}, f32[4,4,256]{2,1,0:T(4,128)S(1)}, s32[4]{0:T(128)S(1)}, bf16[2048,1024]{0,1:T(8,128)(2,1)...) while((s32[]{:T(128)}, ...), condition=%wide.region_13.14_spmd.clone, body=%wide.region_10.13_spmd.clone.sunk | while | flops 562560000 | bytes 34383056 | solution.py:120
  734.7 152.6 %all-gather.40.cloned.1.call-done = bf16[1,1024,5248]{2,1,0:T(8,128)(2,1)} async-done(((bf16[1,128,5248]{2,1,0:T(8,128)(2,1)}), bf16[1,1024,5248]{2,1,0:T(8,128)(2,1)}) %all-gather.40.cloned.1.call-update) | async-done | bytes 10747920 | tf_op jit(solution)/shard_map/all_gather | solution.py:199
  896.3 79.1 %all-gather.42.cloned.1.call-done = bf16[1,2624,1024]{2,1,0:T(8,128)(2,1)} async-done(((bf16[1,328,1024]{2,1,0:T(8,128)(2,1)}), bf16[1,2624,1024]{2,1,0:T(8,128)(2,1)}) %all-gather.42.cloned.1.call-update) | async-done | bytes 5373968 | tf_op jit(solution)/shard_map/all_gather | solution.py:200
  975.4 10.3 fusion.107
  1001.5 104.4 %while.66 = (s32[]{:T(128)}, f32[4,256,256]{1,2,0:T(8,128)}, bf16[4,2048,256]{1,2,0:T(8,128)(2,1)}, bf16[4,2048,256]{1,2,0:T(8,128)(2,1)}, s32[4]{0:T(128)S(1)},...) while((s32[]{:T(128)}, f32[4,256,256]{1,2,0:T(8,128)}, ...), condition=%wide.region_20.21_spmd.clone, body=%wide.region_18.20_spmd.clone.sunk | while | flops 1375271936 | bytes 105944528 | solution.py:167
  1122.8 139.2 %reduce-scatter.10.cloned.1.call-done = bf16[256,2048]{0,1:T(8,128)(2,1)} async-done(((bf16[2048,2048]{0,1:T(8,128)(2,1)}), bf16[256,2048]{0,1:T(8,128)(2,1)}) %reduce-scatter.10.cloned.1.call-update) | async-done | bytes 1048592 | tf_op jit(solution)/shard_map/reduce_scatter | solution.py:313
  1318.1 55.5 %while.67 = (s32[]{:T(128)}, f32[4,256,256]{1,2,0:T(8,128)}, f32[4,1280,256]{1,2,0:T(8,128)}, f32[4,1280,256]{1,2,0:T(8,128)}, s32[4]{0:T(128)S(1)}, /*index=5*/...) while((s32[]{:T(128)}, f32[4,256,256]{1,2,0:T(8,128)}, ...), condition=%wide.region_28.29_spmd.clone, body=%wide.region_26.28_spmd.clone.sunk | while | flops 852687872 | bytes 54567408 | solution.py:167
  1390.9 17.7 collective-permute-done.19
  1408.6 35.6 %collective-permute-done.18 = bf16[256,2048]{0,1:T(8,128)(2,1)S(1)} collective-permute-done((bf16[256,2048]{0,1:T(8,128)(2,1)S(1)}, bf16[256,2048]{0,1:T(8,128)(2,1)S(1)}, u32[]{:S(2)}, u32[]{:S(2)}) %collective-permute-start.18) | collective-permute-done | bytes 1048608 | tf_op jit(solution)/shard_map/ppermute | solution.py:27
  1454.6 9.9 convolution_convert_fusion.1
  1464.6 15.1 reduce-scatter.26.cloned.1.call-done
  1479.7 70.7 %reduce-scatter.16.cloned.1.call-done = bf16[128,1024]{1,0:T(8,128)(2,1)} async-done(((bf16[1024,1024]{1,0:T(8,128)(2,1)}), bf16[128,1024]{1,0:T(8,128)(2,1)}) %reduce-scatter.16.cloned.1.call-update) | async-done | bytes 262160 | tf_op jit(solution)/shard_map/reduce_scatter | solution.py:342
  1550.4 184.3 %reduce-scatter.22.cloned.1.call-done = bf16[128,5248]{1,0:T(8,128)(2,1)} async-done(((bf16[1024,5248]{1,0:T(8,128)(2,1)}), bf16[128,5248]{1,0:T(8,128)(2,1)}) %reduce-scatter.22.cloned.1.call-update) | async-done | bytes 1343504 | tf_op jit(solution)/shard_map/reduce_scatter | solution.py:348
  1734.7 107.5 %reduce-scatter.24.cloned.1.call-done = bf16[328,1024]{1,0:T(8,128)(2,1)} async-done(((bf16[2624,1024]{1,0:T(8,128)(2,1)}), bf16[328,1024]{1,0:T(8,128)(2,1)}) %reduce-scatter.24.cloned.1.call-update) | async-done | bytes 671760 | tf_op jit(solution)/shard_map/reduce_scatter | solution.py:351
  1842.2 121.1 %reduce-scatter.14.cloned.1.call-done = bf16[128,3072]{1,0:T(8,128)(2,1)} async-done(((bf16[1024,3072]{1,0:T(8,128)(2,1)}), bf16[128,3072]{1,0:T(8,128)(2,1)}) %reduce-scatter.14.cloned.1.call-update) | async-done | bytes 786448 | tf_op jit(solution)/shard_map/reduce_scatter | solution.py:339
  1963.3 120.6 %reduce-scatter.12.cloned.1.call-done = bf16[128,3072]{1,0:T(8,128)(2,1)} async-done(((bf16[1024,3072]{1,0:T(8,128)(2,1)}), bf16[128,3072]{1,0:T(8,128)(2,1)}) %reduce-scatter.12.cloned.1.call-update) | async-done | bytes 786448 | tf_op jit(solution)/shard_map/reduce_scatter | solution.py:339
  2083.9 184.6 %reduce-scatter.20.cloned.1.call-done = bf16[128,5248]{1,0:T(8,128)(2,1)} async-done(((bf16[1024,5248]{1,0:T(8,128)(2,1)}), bf16[128,5248]{1,0:T(8,128)(2,1)}) %reduce-scatter.20.cloned.1.call-update) | async-done | bytes 1343504 | tf_op jit(solution)/shard_map/reduce_scatter | solution.py:348
  2281.7 19.1 all-reduce.16
  2310.2 78.6 %all-reduce.21.cloned.1.call-done = (bf16[1,128,3072]{2,1,0:T(8,128)(2,1)}, bf16[1,128,3072]{2,1,0:T(8,128)(2,1)}, bf16[1,128,1024]{2,1,0:T(8,128)(2,1)}, bf16[1...) async-done(((bf16[1,128,3072]{2,1,0:T(8,128)(2,1)}, ...) | async-done | bytes 6127632 | tf_op jit(solution)/shard_map/psum | solution.py:357
  (724 shorter events, 540.1 us)
Async XLA Ops:
  7.2 105.6 %all-gather.28.cloned.1.call-start = ((), (), s32[]{:S(2)}) async-start(), calls=%async_computation.20 | async-start | bytes 7077888 | tf_op jit(solution)/shard_map/all_gather | solution.py:196
  10.0 219.7 %all-gather.30.cloned.1.call-start = ((), (), s32[]{:S(2)}) async-start(), calls=%async_computation.21 | async-start | bytes 2359296 | tf_op jit(solution)/shard_map/all_gather | solution.py:197
  10.9 328.2 %all-gather.32.cloned.1.call-start = ((), (), s32[]{:S(2)}) async-start(), calls=%async_computation.22 | async-start | bytes 12091392 | tf_op jit(solution)/shard_map/all_gather | solution.py:199
  12.8 414.5 %all-gather.34.cloned.1.call-start = ((), (), s32[]{:S(2)}) async-start(), calls=%async_computation.23 | async-start | bytes 6045696 | tf_op jit(solution)/shard_map/all_gather | solution.py:200
  15.4 511.7 %all-gather.36.cloned.1.call-start = ((), (), s32[]{:S(2)}) async-start(), calls=%async_computation.24 | async-start | bytes 7077888 | tf_op jit(solution)/shard_map/all_gather | solution.py:196
  15.5 72.6 %collective-permute-start.8 = (s32[256]{0:T(256)S(1)}, s32[256]{0:T(256)S(1)}, u32[]{:S(2)}, u32[]{:S(2)}) collective-permute-start(s32[256]{0:T(256)S(1)} %copy-done.73), channel_id=1, source_target_pairs={{0,2},{1,3},{2,4},{3,5},{4,6},{5,7},{8,10},{9,11},{10,12},{11,13},... | collective-permute-start | bytes 3080 | tf_op jit(solution)/shard_map/ppermute | solution.py:27
  20.4 69.0 %collective-permute-start.9 = (s32[256]{0:T(256)S(1)}, s32[256]{0:T(256)S(1)}, u32[]{:S(2)}, u32[]{:S(2)}) collective-permute-start(s32[256]{0:T(256)S(1)} %copy-done.73), channel_id=1, source_target_pairs={{0,1},{1,2},{2,3},{3,4},{4,5},{5,6},{6,7},{8,9},{9,10},{10,11},{11... | collective-permute-start | bytes 3080 | tf_op jit(solution)/shard_map/ppermute | solution.py:27
  23.8 67.2 %collective-permute-start.4 = (s32[256]{0:T(256)S(1)}, s32[256]{0:T(256)S(1)}, u32[]{:S(2)}, u32[]{:S(2)}) collective-permute-start(s32[256]{0:T(256)S(1)} %broadcast_add_fusion), channel_id=1, source_target_pairs={{0,2},{1,3},{2,4},{3,5},{4,6},{5,7},{8,10},{9,11},{10,12},{11,13},... | collective-permute-start | bytes 3080 | tf_op jit(solution)/shard_map/ppermute | solution.py:27
  27.3 65.0 %collective-permute-start.5 = (s32[256]{0:T(256)S(1)}, s32[256]{0:T(256)S(1)}, u32[]{:S(2)}, u32[]{:S(2)}) collective-permute-start(s32[256]{0:T(256)S(1)} %broadcast_add_fusion), channel_id=1, source_target_pairs={{0,1},{1,2},{2,3},{3,4},{4,5},{5,6},{6,7},{8,9},{9,10},{10,11},{11... | collective-permute-start | bytes 3080 | tf_op jit(solution)/shard_map/ppermute | solution.py:27
  30.8 61.6 %collective-permute-start.6 = (s32[256]{0:T(256)S(1)}, s32[256]{0:T(256)S(1)}, u32[]{:S(2)}, u32[]{:S(2)}) collective-permute-start(s32[256]{0:T(256)S(1)} %broadcast_add_fusion), channel_id=1, source_target_pairs={{1,0},{2,1},{3,2},{4,3},{5,4},{6,5},{7,6},{9,8},{10,9},{11,10},{12... | collective-permute-start | bytes 3080 | tf_op jit(solution)/shard_map/ppermute | solution.py:27
  32.1 574.1 %all-gather.24.cloned.1.call-start = ((), (), s32[]{:S(2)}) async-start(), calls=%async_computation.9 | async-start | bytes 4718592 | tf_op jit(solution)/shard_map/all_gather | solution.py:218
  125.7 43.0 %collective-permute-start.3 = (bf16[256,1024]{1,0:T(8,128)(2,1)}, bf16[256,1024]{1,0:T(8,128)(2,1)}, u32[]{:S(2)}, u32[]{:S(2)}) collective-permute-start(bf16[256,1024]{1,0:T(8,128)(2,1)} %slice.281), channel_id=1, source_target_pairs={{2,0},{3,1},{4,2},{5,3},{6,4},{7,5},{10,8},{11,9},{12,10},{13,11},... | collective-permute-start | bytes 1572872 | tf_op jit(solution)/shard_map/ppermute | solution.py:27
  131.2 42.4 %collective-permute-start.12 = (bf16[256,1024]{0,1:T(8,128)(2,1)}, bf16[256,1024]{0,1:T(8,128)(2,1)}, u32[]{:S(2)}, u32[]{:S(2)}) collective-permute-start(bf16[256,1024]{0,1:T(8,128)(2,1)} %bitcast.5), channel_id=1, source_target_pairs={{0,2},{1,3},{2,4},{3,5},{4,6},{5,7},{8,10},{9,11},{10,12},{11,13},... | collective-permute-start | bytes 1572872 | tf_op jit(solution)/shard_map/ppermute | solution.py:27
  141.5 33.2 %collective-permute-start.13 = (bf16[256,1024]{0,1:T(8,128)(2,1)}, bf16[256,1024]{0,1:T(8,128)(2,1)}, u32[]{:S(2)}, u32[]{:S(2)}) collective-permute-start(bf16[256,1024]{0,1:T(8,128)(2,1)} %bitcast.5), channel_id=1, source_target_pairs={{0,1},{1,2},{2,3},{3,4},{4,5},{5,6},{6,7},{8,9},{9,10},{10,11},{11... | collective-permute-start | bytes 1572872 | tf_op jit(solution)/shard_map/ppermute | solution.py:27
  155.6 40.1 %collective-permute-start.15 = (bf16[256,1024]{0,1:T(8,128)(2,1)}, bf16[256,1024]{0,1:T(8,128)(2,1)}, u32[]{:S(2)}, u32[]{:S(2)}) collective-permute-start(bf16[256,1024]{0,1:T(8,128)(2,1)} %bitcast.5), channel_id=1, source_target_pairs={{2,0},{3,1},{4,2},{5,3},{6,4},{7,5},{10,8},{11,9},{12,10},{13,11},... | collective-permute-start | bytes 1572872 | tf_op jit(solution)/shard_map/ppermute | solution.py:27
  534.4 147.8 %all-gather.26.cloned.1.call-start = ((), (), s32[]{:S(2)}) async-start(), calls=%async_computation.10 | async-start | bytes 4718592 | tf_op jit(solution)/shard_map/all_gather | solution.py:217
  541.1 190.9 %all-gather.38.cloned.1.call-start = ((), (), s32[]{:S(2)}) async-start(), calls=%async_computation.25 | async-start | bytes 2359296 | tf_op jit(solution)/shard_map/all_gather | solution.py:197
  541.8 345.5 %all-gather.40.cloned.1.call-start = ((), (), s32[]{:S(2)}) async-start(), calls=%async_computation.26 | async-start | bytes 12091392 | tf_op jit(solution)/shard_map/all_gather | solution.py:199
  542.5 432.8 %all-gather.42.cloned.1.call-start = ((), (), s32[]{:S(2)}) async-start(), calls=%async_computation.27 | async-start | bytes 6045696 | tf_op jit(solution)/shard_map/all_gather | solution.py:200
  543.1 718.8 %reduce-scatter.10.cloned.1.call-start = ((), (), s32[]{:S(2)}) async-start(), calls=%async_computation.11 | async-start | bytes 9437184 | tf_op jit(solution)/shard_map/reduce_scatter | solution.py:313
  1114.2 350.3 %reduce-scatter.18.cloned.1.call-start = ((), (), s32[]{:S(2)}) async-start(), calls=%async_computation.15 | async-start | bytes 2359296 | tf_op jit(solution)/shard_map/reduce_scatter | solution.py:342
  1118.4 361.3 %reduce-scatter.26.cloned.1.call-start = ((), (), s32[]{:S(2)}) async-start(), calls=%async_computation.19 | async-start | bytes 6045696 | tf_op jit(solution)/shard_map/reduce_scatter | solution.py:351
  1122.5 427.9 %reduce-scatter.16.cloned.1.call-start = ((), (), s32[]{:S(2)}) async-start(), calls=%async_computation.14 | async-start | bytes 2359296 | tf_op jit(solution)/shard_map/reduce_scatter | solution.py:342
  1291.1 443.7 %reduce-scatter.22.cloned.1.call-start = ((), (), s32[]{:S(2)}) async-start(), calls=%async_computation.17 | async-start | bytes 12091392 | tf_op jit(solution)/shard_map/reduce_scatter | solution.py:348
  1301.4 540.8 %reduce-scatter.24.cloned.1.call-start = ((), (), s32[]{:S(2)}) async-start(), calls=%async_computation.18 | async-start | bytes 6045696 | tf_op jit(solution)/shard_map/reduce_scatter | solution.py:351
  1307.0 656.3 %reduce-scatter.14.cloned.1.call-start = ((), (), s32[]{:S(2)}) async-start(), calls=%async_computation.13 | async-start | bytes 7077888 | tf_op jit(solution)/shard_map/reduce_scatter | solution.py:339
  1314.1 769.8 %reduce-scatter.12.cloned.1.call-start = ((), (), s32[]{:S(2)}) async-start(), calls=%async_computation.12 | async-start | bytes 7077888 | tf_op jit(solution)/shard_map/reduce_scatter | solution.py:339
  1384.9 59.3 %collective-permute-start.18 = (bf16[256,2048]{0,1:T(8,128)(2,1)S(1)}, bf16[256,2048]{0,1:T(8,128)(2,1)S(1)}, u32[]{:S(2)}, u32[]{:S(2)}) collective-permute-start(bf16[256,2048]{0,1:T(8,128)(2,1)S(1)} %get-tuple-element.898), channel_id=1, source_target_pairs={{0,1},{1,2},{2,3},{3,4},{4,5},{5,6},{6,7},{8,9},{9,10},{10,11},{11... | collective-permute-start | bytes 3145736 | tf_op jit(solution)/shard_map/ppermute | solution.py:27
  1388.3 55.9 %collective-permute-start.17 = (bf16[256,2048]{0,1:T(8,128)(2,1)S(1)}, bf16[256,2048]{0,1:T(8,128)(2,1)S(1)}, u32[]{:S(2)}, u32[]{:S(2)}) collective-permute-start(bf16[256,2048]{0,1:T(8,128)(2,1)S(1)} %get-tuple-element.899), channel_id=1, source_target_pairs={{1,0},{2,1},{3,2},{4,3},{5,4},{6,5},{7,6},{9,8},{10,9},{11,10},{12... | collective-permute-start | bytes 3145736 | tf_op jit(solution)/shard_map/ppermute | solution.py:27
  1389.6 54.6 %collective-permute-start.16 = (bf16[256,2048]{0,1:T(8,128)(2,1)S(1)}, bf16[256,2048]{0,1:T(8,128)(2,1)S(1)}, u32[]{:S(2)}, u32[]{:S(2)}) collective-permute-start(bf16[256,2048]{0,1:T(8,128)(2,1)S(1)} %get-tuple-element.896), channel_id=1, source_target_pairs={{2,0},{3,1},{4,2},{5,3},{6,4},{7,5},{10,8},{11,9},{12,10},{13,11},... | collective-permute-start | bytes 3145736 | tf_op jit(solution)/shard_map/ppermute | solution.py:27
  1453.9 814.5 %reduce-scatter.20.cloned.1.call-start = ((), (), s32[]{:S(2)}) async-start(), calls=%async_computation.16 | async-start | bytes 12091392 | tf_op jit(solution)/shard_map/reduce_scatter | solution.py:348
  1464.5 924.3 %all-reduce.21.cloned.1.call-start = ((), (), s32[]{:S(2)}) async-start(), calls=%async_computation.28 | async-start | bytes 12255232 | tf_op jit(solution)/shard_map/psum | solution.py:357
  (155 other events, 6066.3 us)
Sparse Core Ops, SparseCore 0:
  10.8 101.9 all-gather.27
  114.9 61.5 all-gather.29
  178.7 160.4 all-gather.31
  341.2 86.0 all-gather.33
  429.9 97.1 all-gather.35
  534.5 71.6 all-gather.23
  608.9 73.2 all-gather.25
  684.3 47.5 all-gather.37
  734.7 152.5 all-gather.39
  889.3 86.0 all-gather.41
  1114.3 147.5 reduce-scatter.9
  1265.7 66.5 reduce-scatter.17
  1336.9 142.7 reduce-scatter.25
  1483.1 67.2 reduce-scatter.15
  1553.9 180.8 reduce-scatter.21
  1738.6 103.5 reduce-scatter.23
  1845.6 117.6 reduce-scatter.13
  1966.7 117.0 reduce-scatter.11
  2087.5 180.9 reduce-scatter.19
  2271.4 117.3 all-reduce.20
where the time goes:
time: 2410 us; the launch traced here: 2400 us
  waiting for transfers between devices  1740 us (72%)
  matrix products  244 us (10%)
  local copies, waits for them, and re-layouts  146 us (6%)
  blocking collectives  115 us (5%)
  other arithmetic  79.5 us (3%)
  starting transfers between devices  51.4 us (2%)
    reduce_scatter x2, waiting for transfers between devices, on_device(): lax.psum_scatter(grad_w_in.astype(jnp.bfloat16), 'fsdp', scatter_dimensio...  369 us
    all_gather x2, waiting for transfers between devices, on_device(): lax.all_gather(w_in[layer_index], 'fsdp', axis=0, tiled=True)  257 us
    reduce_scatter x2, waiting for transfers between devices, on_device(): lax.psum_scatter(grad_w_qkv.astype(jnp.bfloat16), 'fsdp', scatter_dimensi...  242 us
    all_gather x2, waiting for transfers between devices, on_device(): lax.all_gather(w_down[layer_index], 'fsdp', axis=0, tiled=True)  151 us
    reduce_scatter x1, waiting for transfers between devices, on_device(): lax.psum_scatter(jnp.concatenate([grad_keys, grad_values], axis=1).astype...  139 us
    reduce_scatter x2, waiting for transfers between devices, on_device(): lax.psum_scatter(grad_w_down.astype(jnp.bfloat16), 'fsdp', scatter_dimens...  123 us
    all_gather x2, waiting for transfers between devices, on_device(): lax.all_gather(w_qkv[layer_index], 'fsdp', axis=0, tiled=True)  110 us
    ppermute x20, waiting for transfers between devices, shifted(): lax.ppermute(value, axis, [(source, source + steps) for source in range(f...  92.6 us
  transfers between devices with their start and end apart: 40, of which 27 were waited for; matrix products, arithmetic and copies ran while one was open for 13% of the time, Pallas kernels for 0%

commit v1 on v0

v1 whole, which is shorter than its diff:
```python
import jax
import jax.numpy as jnp
from jax import lax
from jax.sharding import PartitionSpec as P

D = 1024
HEADS = 16
HEAD_DIM = 64
FF = 2624
HALF_WINDOW = 64
LAYERS = 2


LOCAL_THETA = 10000.0
GLOBAL_THETA = 160000.0
MASKED_SCORE = -1e30
NORM_EPSILON = 1e-05


def shifted(value, axis, steps):
    count = lax.axis_size(axis)
    first, last = (max(0, -steps), min(count, count - steps))
    return lax.ppermute(value, axis, [(source, source + steps) for source in range(first, last)])


def layer_norm(values, gain_row):
    center = values - jnp.mean(values, axis=-1, keepdims=True)
    spread = jnp.mean(center * center, axis=-1, keepdims=True)
    return center * lax.rsqrt(spread + NORM_EPSILON) * gain_row


def rotate(matrix, places, base_theta):
    row_count = matrix.shape[0]
    shaped = matrix.reshape(row_count, HEADS, HEAD_DIM)
    half_dim = HEAD_DIM // 2
    frequency = jnp.power(base_theta, -2.0 * jnp.arange(half_dim, dtype=jnp.float32) / HEAD_DIM)
    angles = places.astype(jnp.float32)[:, None] * frequency[None, :]
    cosine = jnp.cos(angles)[:, None, :]
    sine_part = jnp.sin(angles)[:, None, :]
    first_half = shaped[..., :half_dim]
    second_half = shaped[..., half_dim:]
    turned = jnp.concatenate(
        [
            first_half * cosine - second_half * sine_part,
            second_half * cosine + first_half * sine_part,
        ],
        axis=-1,
    )
    return turned.reshape(row_count, HEADS * HEAD_DIM)


def rotate_back(gradient, places, base_theta):
    turned, pull_back = jax.vjp(lambda rotated_in: rotate(rotated_in, places, base_theta), gradient)
    return pull_back(gradient)[0]


def gelu_gate(raised):
    return jax.nn.gelu(raised[:, :FF], approximate=False) * raised[:, FF:]


def contract_rows(left, right):
    return lax.dot_general(
        left, right, (((0,), (0,)), ((), ())), preferred_element_type=jnp.float32
    )


def contract_cols(left, right):
    return lax.dot_general(
        left, right, (((1,), (1,)), ((), ())), preferred_element_type=jnp.float32
    )


def head_block(matrix, group_index, head_width):
    columns = lax.dynamic_slice_in_dim(
        matrix, group_index * head_width * HEAD_DIM, head_width * HEAD_DIM, 1
    )
    return columns.reshape(matrix.shape[0], head_width, HEAD_DIM)


def merge_heads(stacked):
    return jnp.transpose(stacked, (1, 0, 2)).reshape(stacked.shape[1], HEADS * HEAD_DIM)


def attend_forward(queries, key_rows, value_rows, allowed):
    head_width = min(4, HEADS)
    score_scale = HEAD_DIM ** (-0.5)

    def one_group(group_index):
        query_block = head_block(queries, group_index, head_width)
        key_block = head_block(key_rows, group_index, head_width)
        value_block = head_block(value_rows, group_index, head_width)
        scores = (
            jnp.einsum("qhd,khd->hqk", query_block, key_block, preferred_element_type=jnp.float32)
            * score_scale
        )
        scores = jnp.where(allowed[None], scores, MASKED_SCORE)
        highest = jnp.max(scores, axis=-1, keepdims=True)
        raised = jnp.exp(scores - highest)
        totals = jnp.sum(raised, axis=-1, keepdims=True)
        soft_weights = (raised / totals).astype(jnp.bfloat16)
        outputs = jnp.einsum(
            "hqk,khd->qhd", soft_weights, value_block, preferred_element_type=jnp.float32
        )
        return (
            outputs.reshape(outputs.shape[0], head_width * HEAD_DIM),
            (highest + jnp.log(totals))[..., 0],
        )

    outputs, log_sums = lax.map(one_group, jnp.arange(HEADS // head_width, dtype=jnp.int32))
    return (merge_heads(outputs), log_sums)


def attend_backward(queries, key_rows, value_rows, grad_mixed, log_sums, allowed):
    head_width = min(4, HEADS)
    score_scale = HEAD_DIM ** (-0.5)

    def one_group(carried):
        group_index, group_sums = carried
        query_block = head_block(queries, group_index, head_width)
        key_block = head_block(key_rows, group_index, head_width)
        value_block = head_block(value_rows, group_index, head_width)
        grad_block = head_block(grad_mixed, group_index, head_width)
        scores = (
            jnp.einsum("qhd,khd->hqk", query_block, key_block, preferred_element_type=jnp.float32)
            * score_scale
        )
        scores = jnp.where(allowed[None], scores, MASKED_SCORE)
        soft_weights = jnp.exp(scores - group_sums[..., None])
        grad_soft = jnp.einsum(
            "qhd,khd->hqk", grad_block, value_block, preferred_element_type=jnp.float32
        )
        inner_sum = jnp.sum(soft_weights * grad_soft, axis=-1, keepdims=True)
        grad_scores = (soft_weights * (grad_soft - inner_sum)).astype(jnp.bfloat16)
        grad_query = (
            jnp.einsum("hqk,khd->qhd", grad_scores, key_block, preferred_element_type=jnp.float32)
            * score_scale
        )
        grad_query = grad_query.reshape(grad_query.shape[0], head_width * HEAD_DIM)
        grad_key = (
            jnp.einsum("hqk,qhd->khd", grad_scores, query_block, preferred_element_type=jnp.float32)
            * score_scale
        )
        grad_value = jnp.einsum(
            "hqk,qhd->khd",
            soft_weights.astype(jnp.bfloat16),
            grad_block,
            preferred_element_type=jnp.float32,
        )
        return (
            grad_query,
            grad_key.reshape(grad_key.shape[0], head_width * HEAD_DIM),
            grad_value.reshape(grad_value.shape[0], head_width * HEAD_DIM),
            inner_sum[..., 0],
        )

    results = lax.map(one_group, (jnp.arange(HEADS // head_width, dtype=jnp.int32), log_sums))
    return (merge_heads(results[0]), merge_heads(results[1]), merge_heads(results[2]), results[3])


def swap(value, bit):
    count = lax.axis_size("rep")
    return lax.ppermute(value, "rep", [(source, source ^ bit) for source in range(count)])


def swap_core(value):
    return swap(value, 1)


def swap_plane(value):
    return swap(value, 2)


def ordered(flag, own, other):
    return (jnp.where(flag == 0, own, other), jnp.where(flag == 0, other, own))


def gather_rows(shard, core):
    half = shard.shape[0] // 2
    own = lax.all_gather(
        lax.dynamic_slice_in_dim(shard, core * half, half, 0), "fsdp", axis=0, tiled=True
    )
    low, high = ordered(core, own, swap_core(own))
    width = shard.shape[1]
    pair = [part.reshape(-1, 1, half, width) for part in (low, high)]
    return jnp.concatenate(pair, axis=1).reshape(-1, width)


def gather_columns(shard, core):
    half = shard.shape[1] // 2
    own = lax.all_gather(
        lax.dynamic_slice_in_dim(shard, core * half, half, 1), "fsdp", axis=0, tiled=True
    )
    return jnp.concatenate(ordered(core, own, swap_core(own)), axis=1)


def halve(parts, flag, exchange):
    kept = lax.dynamic_index_in_dim(parts, flag, 1, keepdims=False)
    sent = lax.dynamic_index_in_dim(parts, 1 - flag, 1, keepdims=False)
    return (kept.astype(jnp.float32) + exchange(sent).astype(jnp.float32)).astype(jnp.bfloat16)


def reduce_rows(gradient, core, plane):
    count = lax.axis_size("fsdp")
    rows, width = gradient.shape
    piece = rows // count // 4
    parts = gradient.astype(jnp.bfloat16).reshape(count * 2, 2, piece, width)
    parts = halve(parts, core, swap_core).reshape(count, 2, piece, width)
    parts = halve(parts, plane, swap_plane).reshape(count * piece, width)
    own = lax.psum_scatter(parts, "fsdp", scatter_dimension=0, tiled=True)
    return lax.all_gather(own, "rep", axis=0, tiled=True).astype(jnp.float32)


def halve_columns(value, flag, exchange):
    half = value.shape[1] // 2
    kept = lax.dynamic_slice_in_dim(value, flag * half, half, 1)
    sent = lax.dynamic_slice_in_dim(value, (1 - flag) * half, half, 1)
    return (kept.astype(jnp.float32) + exchange(sent).astype(jnp.float32)).astype(jnp.bfloat16)


def reduce_columns(gradient, core, plane):
    parts = halve_columns(gradient.astype(jnp.bfloat16), core, swap_core)
    parts = halve_columns(parts, plane, swap_plane)
    own = lax.psum_scatter(parts, "fsdp", scatter_dimension=0, tiled=True)
    every = lax.all_gather(own, "rep", axis=0, tiled=False)
    return jnp.concatenate([every[0], every[2], every[1], every[3]], axis=1).astype(jnp.float32)


def on_device(
    tokens, segment_ids, positions, attn_gain, w_qkv, w_out, mlp_gain, w_in, w_down, cotangent
):
    row_count = tokens.shape[0]
    member = lax.axis_index("rep")
    core, plane = (member % 2, member // 2)
    place = lax.axis_index("fsdp")
    hops = -(-HALF_WINDOW // (row_count // 4))
    offsets = [step for step in range(-hops, hops + 1)]
    shard_rows = attn_gain.shape[1]
    half_rows = shard_rows // 2

    gains = jnp.concatenate([attn_gain, mlp_gain], axis=0)
    first = lax.dynamic_slice_in_dim(w_qkv[0], core * half_rows, half_rows, 0)
    gain_block = jnp.pad(gains, ((0, half_rows - 2 * LAYERS), (0, 0)))
    own = lax.all_gather(
        jnp.concatenate([first, gain_block], axis=1), "fsdp", axis=0, tiled=True
    )
    low, high = ordered(core, own[:, : 3 * D], swap_core(own[:, : 3 * D]))
    pair = [part.reshape(-1, 1, half_rows, 3 * D) for part in (low, high)]
    qkv_first = jnp.concatenate(pair, axis=1).reshape(D, 3 * D)
    all_gains = own[:, 3 * D :].reshape(-1, half_rows, shard_rows)[:, : 2 * LAYERS]
    all_gains = jnp.transpose(all_gains, (1, 0, 2)).reshape(2 * LAYERS, D).astype(jnp.float32)

    marks = lax.all_gather(jnp.stack([segment_ids, positions]), "fsdp", axis=1, tiled=True)
    padded = jnp.pad(marks, ((0, 0), (hops * row_count, hops * row_count)), constant_values=-1)
    near = lax.dynamic_slice_in_dim(padded, place * row_count, len(offsets) * row_count, 1)
    allowed_near = (segment_ids[:, None] == near[0][None, :]) & (
        jnp.abs(positions[:, None] - near[1][None, :]) <= HALF_WINDOW
    )
    allowed_all = segment_ids[:, None] == marks[0][None, :]

    out_first = gather_rows(w_out[0], core)
    in_first = gather_rows(w_in[0], core)
    down_first = gather_columns(w_down[0], core)
    both = gather_rows(jnp.concatenate([w_qkv[1], w_out[1]], axis=1), core)
    matrices = (
        (qkv_first, out_first, in_first, down_first),
        (both[:, : 3 * D], both[:, 3 * D :], gather_rows(w_in[1], core), gather_columns(w_down[1], core)),
    )

    hidden = tokens.astype(jnp.float32)
    memory = []
    for layer_index in range(LAYERS):
        base_theta = LOCAL_THETA if layer_index == 0 else GLOBAL_THETA
        mat_qkv, mat_out, mat_in, mat_down = matrices[layer_index]
        normed = layer_norm(hidden, all_gains[layer_index]).astype(jnp.bfloat16)
        projected = jnp.dot(normed, mat_qkv, preferred_element_type=jnp.float32)
        queries = rotate(projected[:, :D], positions, base_theta).astype(jnp.bfloat16)
        pairs = jnp.concatenate(
            [
                rotate(projected[:, D : 2 * D], positions, base_theta).astype(jnp.bfloat16),
                projected[:, 2 * D :].astype(jnp.bfloat16),
            ],
            axis=1,
        )
        if layer_index == 0:
            rows = jnp.concatenate(
                [pairs if step == 0 else shifted(pairs, "fsdp", -step) for step in offsets], axis=0
            )
            allowed = allowed_near
        else:
            rows = lax.all_gather(pairs, "fsdp", axis=0, tiled=True)
            allowed = allowed_all
        key_rows, value_rows = (rows[:, :D], rows[:, D:])
        attended, log_sums = attend_forward(queries, key_rows, value_rows, allowed)
        attended = attended.astype(jnp.bfloat16)
        middle = hidden + jnp.dot(attended, mat_out, preferred_element_type=jnp.float32)
        normed_mlp = layer_norm(middle, all_gains[LAYERS + layer_index]).astype(jnp.bfloat16)
        raised = jnp.dot(normed_mlp, mat_in, preferred_element_type=jnp.float32)
        gated_hidden = gelu_gate(raised).astype(jnp.bfloat16)
        output = middle + jnp.dot(gated_hidden, mat_down, preferred_element_type=jnp.float32)
        memory.append(
            (
                hidden,
                normed,
                queries,
                key_rows,
                value_rows,
                allowed,
                attended,
                log_sums,
                middle,
                normed_mlp,
                raised,
                gated_hidden,
            )
        )
        hidden = output
    grad_hidden = cotangent.astype(jnp.float32)
    owned = [None, None]
    gain_rows = [None] * (2 * LAYERS)
    for layer_index in range(LAYERS - 1, -1, -1):
        base_theta = LOCAL_THETA if layer_index == 0 else GLOBAL_THETA
        (
            layer_input,
            normed,
            queries,
            key_rows,
            value_rows,
            allowed,
            attended,
            log_sums,
            middle,
            normed_mlp,
            raised,
            gated_hidden,
        ) = memory[layer_index]
        mat_qkv, mat_out, mat_in, mat_down = matrices[layer_index]
        grad_branch = grad_hidden.astype(jnp.bfloat16)
        own_down = reduce_columns(contract_rows(gated_hidden, grad_branch), core, plane)
        grad_gated = contract_cols(grad_branch, mat_down)
        unused, pull_gate = jax.vjp(gelu_gate, raised)
        grad_raised = pull_gate(grad_gated)[0].astype(jnp.bfloat16)
        own_in = reduce_rows(contract_rows(normed_mlp, grad_raised), core, plane)
        grad_normed_mlp = contract_cols(grad_raised, mat_in)
        unused, pull_norm = jax.vjp(layer_norm, middle, all_gains[LAYERS + layer_index])
        grad_middle_part, gain_rows[LAYERS + layer_index] = pull_norm(grad_normed_mlp)
        grad_middle = grad_hidden + grad_middle_part
        grad_attn_in = grad_middle.astype(jnp.bfloat16)
        own_out = reduce_rows(contract_rows(attended, grad_attn_in), core, plane)
        grad_mixed = contract_cols(grad_attn_in, mat_out).astype(jnp.bfloat16)
        grad_queries, grad_keys, grad_values, inner = attend_backward(
            queries, key_rows, value_rows, grad_mixed, log_sums, allowed
        )
        pair_grads = jnp.concatenate([grad_keys, grad_values], axis=1)
        if layer_index == 0:
            window_grads = pair_grads.reshape(len(offsets), row_count, 2 * D)
            summed = window_grads[hops]
            for slot, step in enumerate(offsets):
                if step != 0:
                    piece = window_grads[slot].astype(jnp.bfloat16)
                    summed = summed + shifted(piece, "fsdp", step).astype(jnp.float32)
        else:
            summed = lax.psum_scatter(
                pair_grads.astype(jnp.bfloat16), "fsdp", scatter_dimension=0, tiled=True
            ).astype(jnp.float32)
        grad_projected = jnp.concatenate(
            [
                rotate_back(grad_queries, positions, base_theta),
                rotate_back(summed[:, :D], positions, base_theta),
                summed[:, D:],
            ],
            axis=1,
        ).astype(jnp.bfloat16)
        own_qkv = reduce_rows(contract_rows(normed, grad_projected), core, plane)
        grad_normed = contract_cols(grad_projected, mat_qkv)
        unused, pull_first = jax.vjp(layer_norm, layer_input, all_gains[layer_index])
        grad_hidden_part, gain_rows[layer_index] = pull_first(grad_normed)
        grad_hidden = grad_middle + grad_hidden_part
        owned[layer_index] = (own_qkv, own_out, own_in, own_down)
    gain_sums = lax.psum(jnp.stack(gain_rows), ("rep", "fsdp"))
    gain_own = lax.dynamic_slice_in_dim(gain_sums, place * shard_rows, shard_rows, 1)
    grads = [jnp.stack([owned[0][index], owned[1][index]]) for index in range(4)]
    return (
        hidden.astype(jnp.bfloat16),
        grad_hidden,
        gain_own[:LAYERS],
        grads[0],
        grads[1],
        gain_own[LAYERS:],
        grads[2],
        grads[3],
    )


def solution(mesh):
    return jax.shard_map(
        on_device,
        mesh=mesh,
        in_specs=(
            P(("rep", "fsdp"), None),
            P(("rep", "fsdp")),
            P(("rep", "fsdp")),
            P(None, "fsdp"),
            P(None, "fsdp", None),
            P(None, "fsdp", None),
            P(None, "fsdp"),
            P(None, "fsdp", None),
            P(None, "fsdp", None),
            P(("rep", "fsdp"), None),
        ),
        out_specs=(
            P(("rep", "fsdp"), None),
            P(("rep", "fsdp"), None),
            P(None, "fsdp"),
            P(None, "fsdp", None),
            P(None, "fsdp", None),
            P(None, "fsdp"),
            P(None, "fsdp", None),
            P(None, "fsdp", None),
        ),
        check_vma=False,
    )
```

time: 2410 us -> 1590 us (0.66)
  waiting for transfers between devices: 1740 us -> 847 us
  other arithmetic: 79.5 us -> 195 us
  matrix products: 244 us -> 201 us
  local copies, waits for them, and re-layouts: 146 us -> 172 us
  starting transfers between devices: 51.4 us -> 25.9 us
    reduce_scatter x9, waiting for transfers between devices: 943 us -> 235 us  [the longest x6 117 us: reduce_rows(): own = lax.psum_scatter(parts, 'fsdp', scatter_dimension=0, tiled=True)]
    all_gather x10, waiting for transfers between devices: 624 us -> 462 us  [the longest x4 172 us: gather_rows(): lax.all_gather(lax.dynamic_slice_in_dim(shard, core * half, half, 0), 'fs...]
    ppermute x0 -> x23, waiting for transfers between devices: none -> 118 us  [swap(): lax.ppermute(value, 'rep', [(source, source ^ bit) for source in range(co...]
    psum x1 -> x0, waiting for transfers between devices: 78.6 us -> none  [on_device(): lax.psum(shares[1].astype(jnp.bfloat16), 'rep').astype(jnp.float32)]
    ppermute x20 -> x4, waiting for transfers between devices: 92.6 us -> 32.2 us  [shifted(): lax.ppermute(value, axis, [(source, source + steps) for source in range(f...]
    convert_element_type x4 -> x18, other arithmetic: 0.02 us -> 49.4 us  [the longest x12 39.3 us: halve(): (kept.astype(jnp.float32) + exchange(sent).astype(jnp.float32)).astype(jn...]
    select_n x0 -> x7, other arithmetic: none -> 39.1 us  [ordered(): return (jnp.where(flag == 0, own, other), jnp.where(flag == 0, other, own))]
    ppermute x20 -> x4, starting transfers between devices: 49.5 us -> 11.7 us  [shifted(): lax.ppermute(value, axis, [(source, source + steps) for source in range(f...]
  transfers between devices with their start and end apart: 40 -> 46, of which waited for: 27 -> 23; matrix products, arithmetic and copies ran while one was open for 13% -> 21% of each run, Pallas kernels for 0% -> 0%
where the time goes in v1:
time: 1590 us
  waiting for transfers between devices  847 us (53%)
  matrix products  201 us (13%)
  other arithmetic  195 us (12%)
  local copies, waits for them, and re-layouts  172 us (11%)
  blocking collectives  116 us (7%)
  starting transfers between devices  25.9 us (2%)
  between operations  16.6 us (1%)
    all_gather x4, waiting for transfers between devices, gather_rows(): lax.all_gather(lax.dynamic_slice_in_dim(shard, core * half, half, 0), 'fs...  172 us
    ppermute x23, waiting for transfers between devices, swap(): lax.ppermute(value, 'rep', [(source, source ^ bit) for source in range(co...  118 us
    reduce_scatter x6, waiting for transfers between devices, reduce_rows(): own = lax.psum_scatter(parts, 'fsdp', scatter_dimension=0, tiled=True)  117 us
    all_gather x2, waiting for transfers between devices, gather_columns(): lax.all_gather(lax.dynamic_slice_in_dim(shard, core * half, half, 1), 'fs...  107 us
    all_gather x1, waiting for transfers between devices, on_device(): rows = lax.all_gather(pairs, 'fsdp', axis=0, tiled=True)  96.7 us
    reduce_scatter x1, waiting for transfers between devices, on_device(): lax.psum_scatter(pair_grads.astype(jnp.bfloat16), 'fsdp', scatter_dimensi...  85.5 us
    all_gather x1, waiting for transfers between devices, on_device(): lax.all_gather(jnp.concatenate([first, gain_block], axis=1), 'fsdp', axis...  58.1 us
    dot_general x8, matrix products, contract_cols(): lax.dot_general(left, right, (((1,), (1,)), ((), ())), preferred_element_...  50.2 us
  transfers between devices with their start and end apart: 46, of which 23 were waited for; matrix products, arithmetic and copies ran while one was open for 21% of the time, Pallas kernels for 0%

profile of v1, /device:TPU:0, one launch (start us, length us, event | category | flops | bytes accessed | tf_op | source)
XLA Modules:
  0.0 1585.1 jit_solution(15091733841025969357)
XLA Ops:
  17.4 58.1 %all-gather.18.cloned.1.call-done = bf16[512,3200]{1,0:T(8,128)(2,1)} async-done(((bf16[64,3200]{1,0:T(8,128)(2,1)}), bf16[512,3200]{1,0:T(8,128)(2,1)}) %all-gather.18.cloned.1.call-update) | async-done | bytes 3276816 | tf_op jit(solution)/shard_map/all_gather | solution.py:243
  81.7 26.2 %all_gather.58 = s32[2,2048]{1,0:T(2,128)S(1)} all-gather(s32[2,256]{1,0:T(2,128)S(1)} %pad_add_fusion), channel_id=1, replica_groups=mesh['rep'=4,'fsdp'=8] {'fsdp'}, dimensions={1}, use_global_device_ids=true | all-gather | bytes 18432 | tf_op jit(solution)/shard_map/all_gather | solution.py:252
  108.1 9.0 all-gather.28.cloned.1.call-done
  122.8 51.2 %all-gather.32.cloned.1.call-done = bf16[1,2624,512]{2,1,0:T(8,128)(2,1)} async-done(((bf16[1,328,512]{2,1,0:T(8,128)(2,1)}), bf16[1,2624,512]{2,1,0:T(8,128)(2,1)}) %all-gather.32.cloned.1.call-update) | async-done | bytes 2686992 | tf_op jit(solution)/shard_map/all_gather | solution.py:190
  174.6 73.9 %all-gather.20.cloned.1.call-done = bf16[512,4096]{1,0:T(8,128)(2,1)} async-done(((bf16[64,4096]{1,0:T(8,128)(2,1)}), bf16[512,4096]{1,0:T(8,128)(2,1)}) %all-gather.20.cloned.1.call-update) | async-done | bytes 4194320 | tf_op jit(solution)/shard_map/all_gather | solution.py:179
  271.9 88.1 %all-gather.30.cloned.1.call-done = bf16[1,512,5248]{2,1,0:T(8,128)(2,1)} async-done(((bf16[1,64,5248]{2,1,0:T(8,128)(2,1)}), bf16[1,512,5248]{2,1,0:T(8,128)(2,1)}) %all-gather.30.cloned.1.call-update) | async-done | bytes 5373968 | tf_op jit(solution)/shard_map/all_gather | solution.py:179
  366.2 24.5 %while.64 = (s32[]{:T(128)}, bf16[4,256,256]{1,2,0:T(8,128)(2,1)}, f32[4,4,256]{2,1,0:T(4,128)S(1)}, s32[4]{0:T(128)S(1)}, bf16[768,1024]{0,1:T(8,128)(2,1)S(1)}...) while((s32[]{:T(128)}, bf16[4,256,256]{1,2,0:T(8,128)(2,1)}, ...), condition=%wide.region_5.6_spmd.clone, body=%wide.region_2.5_spmd.clone.sunk | while | flops 211745792 | bytes 13410527 | solution.py:109
  408.9 9.2 broadcast_select_fusion.3
  448.1 55.7 %all-gather.36.cloned.1.call-done = bf16[1,2624,512]{2,1,0:T(8,128)(2,1)} async-done(((bf16[1,328,512]{2,1,0:T(8,128)(2,1)}), bf16[1,2624,512]{2,1,0:T(8,128)(2,1)}) %all-gather.36.cloned.1.call-update) | async-done | bytes 2686992 | tf_op jit(solution)/shard_map/all_gather | solution.py:190
  514.6 9.3 broadcast_select_fusion.1
  523.9 9.5 pad_maximum_fusion.1
  533.4 96.7 %all-gather.22.cloned.1.call-done = bf16[2048,2048]{1,0:T(8,128)(2,1)} async-done(((bf16[256,2048]{1,0:T(8,128)(2,1)}), bf16[2048,2048]{1,0:T(8,128)(2,1)}) %all-gather.22.cloned.1.call-update) | async-done | bytes 8388624 | tf_op jit(solution)/shard_map/all_gather | solution.py:290
  649.2 40.8 %while.65 = (s32[]{:T(128)}, bf16[4,256,256]{1,2,0:T(8,128)(2,1)S(1)}, f32[4,4,256]{2,1,0:T(4,128)S(1)}, s32[4]{0:T(128)S(1)}, bf16[2048,1024]{0,1:T(8,128)(2,1)...) while((s32[]{:T(128)}, ...), condition=%wide.region_13.14_spmd.clone, body=%wide.region_10.13_spmd.clone.sunk | while | flops 562560000 | bytes 34383056 | solution.py:109
  699.4 9.7 fusion.88
  727.8 98.7 %while.66 = (s32[]{:T(128)}, f32[4,256,256]{1,2,0:T(8,128)}, bf16[4,2048,256]{1,2,0:T(8,128)(2,1)}, bf16[4,2048,256]{1,2,0:T(8,128)(2,1)}, s32[4]{0:T(128)S(1)},...) while((s32[]{:T(128)}, f32[4,256,256]{1,2,0:T(8,128)}, ...), condition=%wide.region_20.21_spmd.clone, body=%wide.region_18.20_spmd.clone.sunk | while | flops 1375271936 | bytes 105944344 | solution.py:156
  826.5 8.3 pad_maximum_fusion.3
  865.7 12.5 collective-permute-done.18
  897.2 85.5 %reduce-scatter.10.cloned.1.call-done = bf16[256,2048]{0,1:T(8,128)(2,1)} async-done(((bf16[2048,2048]{0,1:T(8,128)(2,1)}), bf16[256,2048]{0,1:T(8,128)(2,1)}) %reduce-scatter.10.cloned.1.call-update) | async-done | bytes 1048592 | tf_op jit(solution)/shard_map/reduce_scatter | solution.py:362
  1020.0 13.0 multiply_reduce_fusion.3
  1046.3 47.7 %while.67 = (s32[]{:T(128)}, f32[4,256,256]{1,2,0:T(8,128)}, f32[4,768,256]{1,2,0:T(8,128)}, f32[4,768,256]{1,2,0:T(8,128)}, s32[4]{0:T(128)S(1)}, /*index=5*/bf...) while((s32[]{:T(128)}, f32[4,256,256]{1,2,0:T(8,128)}, ...), condition=%wide.region_28.29_spmd.clone, body=%wide.region_26.28_spmd.clone.sunk | while | flops 511638528 | bytes 33583360 | solution.py:156
  1122.8 32.2 %collective-permute-done.10 = bf16[256,2048]{0,1:T(8,128)(2,1)S(1)} collective-permute-done((bf16[256,2048]{0,1:T(8,128)(2,1)}, bf16[256,2048]{0,1:T(8,128)(2,1)S(1)}, u32[]{:S(2)}, u32[]{:S(2)}) %collective-permute-start.10) | collective-permute-done | bytes 1048608 | tf_op jit(solution)/shard_map/ppermute | solution.py:23
  1181.9 20.4 %collective-permute-done.24 = bf16[2624,256]{1,0:T(8,128)(2,1)} collective-permute-done((bf16[2624,256]{1,0:T(8,128)(2,1)}, bf16[2624,256]{1,0:T(8,128)(2,1)}, u32[]{:S(2)}, u32[]{:S(2)}) %collective-permute-start.24) | collective-permute-done | bytes 1343520 | tf_op jit(solution)/shard_map/ppermute | solution.py:162
  1208.0 33.6 %collective-permute-done.14 = bf16[8,32,3072]{2,1,0:T(8,128)(2,1)S(1)} collective-permute-done((bf16[8,32,3072]{2,1,0:T(8,128)(2,1)S(1)}, bf16[8,32,3072]{2,1,0:T(8,128)(2,1)S(1)}, u32[]{:S(2)}, u32[]{:S(2)}) %collective-permute-start.14) | collective-permute-done | bytes 1572896 | tf_op jit(solution)/shard_map/ppermute | solution.py:162
  1249.5 32.5 %collective-permute-done.12 = bf16[8,32,3072]{2,1,0:T(8,128)(2,1)S(1)} collective-permute-done((bf16[8,32,3072]{2,1,0:T(8,128)(2,1)S(1)}, bf16[8,32,3072]{2,1,0:T(8,128)(2,1)S(1)}, u32[]{:S(2)}, u32[]{:S(2)}) %collective-permute-start.12) | collective-permute-done | bytes 1572896 | tf_op jit(solution)/shard_map/ppermute | solution.py:162
  1295.5 8.3 all-gather.6
  1310.9 42.0 %psum.7 = f32[4,1024]{1,0:T(4,128)} all-reduce(f32[4,1024]{1,0:T(4,128)} %pad_maximum_fusion.33), channel_id=1, replica_groups=mesh['rep'=4,'fsdp'=8] {'rep','fsdp'}, use_global_device_ids=true, to_apply=%region_35.36 | all-reduce | flops 4096 | bytes 32768 | tf_op jit(solution)/shard_map/psum | solution.py:379
  1366.7 32.5 %reduce-scatter.24.cloned.1.call-done = bf16[328,256]{1,0:T(8,128)(2,1)} async-done(((bf16[2624,256]{1,0:T(8,128)(2,1)}), bf16[328,256]{1,0:T(8,128)(2,1)}) %reduce-scatter.24.cloned.1.call-update) | async-done | bytes 167952 | tf_op jit(solution)/shard_map/reduce_scatter | solution.py:223
  1409.3 57.8 %reduce-scatter.14.cloned.1.call-done = bf16[32,3072]{1,0:T(8,128)(2,1)} async-done(((bf16[256,3072]{1,0:T(8,128)(2,1)}), bf16[32,3072]{1,0:T(8,128)(2,1)}) %reduce-scatter.14.cloned.1.call-update) | async-done | bytes 196624 | tf_op jit(solution)/shard_map/reduce_scatter | solution.py:209
  1467.2 8.8 all_gather.67
  1476.0 58.8 %reduce-scatter.12.cloned.1.call-done = bf16[32,3072]{1,0:T(8,128)(2,1)} async-done(((bf16[256,3072]{1,0:T(8,128)(2,1)}), bf16[32,3072]{1,0:T(8,128)(2,1)}) %reduce-scatter.12.cloned.1.call-update) | async-done | bytes 196624 | tf_op jit(solution)/shard_map/reduce_scatter | solution.py:209
  1534.8 8.7 all_gather.66
  1553.6 20.0 %all-gather.24.cloned.1.call-done = bf16[128,5248]{1,0:T(8,128)(2,1)} async-done(((bf16[32,5248]{1,0:T(8,128)(2,1)}), bf16[128,5248]{1,0:T(8,128)(2,1)}) %all-gather.24.cloned.1.call-update) | async-done | bytes 1343504 | tf_op jit(solution)/shard_map/all_gather | solution.py:210
  (763 shorter events, 585.2 us)
Async XLA Ops:
  7.2 68.3 %all-gather.18.cloned.1.call-start = ((), (), s32[]{:S(2)}) async-start(), calls=%async_computation.9 | async-start | bytes 3686400 | tf_op jit(solution)/shard_map/all_gather | solution.py:243
  9.7 107.3 %all-gather.28.cloned.1.call-start = ((), (), s32[]{:S(2)}) async-start(), calls=%async_computation.23 | async-start | bytes 1179648 | tf_op jit(solution)/shard_map/all_gather | solution.py:179
  11.6 162.4 %all-gather.32.cloned.1.call-start = ((), (), s32[]{:S(2)}) async-start(), calls=%async_computation.25 | async-start | bytes 3022848 | tf_op jit(solution)/shard_map/all_gather | solution.py:190
  12.5 236.0 %all-gather.20.cloned.1.call-start = ((), (), s32[]{:S(2)}) async-start(), calls=%async_computation.10 | async-start | bytes 4718592 | tf_op jit(solution)/shard_map/all_gather | solution.py:179
  13.4 346.6 %all-gather.30.cloned.1.call-start = ((), (), s32[]{:S(2)}) async-start(), calls=%async_computation.24 | async-start | bytes 6045696 | tf_op jit(solution)/shard_map/all_gather | solution.py:179
  16.3 431.8 %all-gather.34.cloned.1.call-start = ((), (), s32[]{:S(2)}) async-start(), calls=%async_computation.26 | async-start | bytes 6045696 | tf_op jit(solution)/shard_map/all_gather | solution.py:179
  17.3 486.5 %all-gather.36.cloned.1.call-start = ((), (), s32[]{:S(2)}) async-start(), calls=%async_computation.27 | async-start | bytes 3022848 | tf_op jit(solution)/shard_map/all_gather | solution.py:190
  79.2 169.3 %collective-permute-start = (bf16[512,3072]{1,0:T(8,128)(2,1)}, bf16[512,3072]{1,0:T(8,128)(2,1)}, u32[]{:S(2)}, u32[]{:S(2)}) collective-permute-start(bf16[512,3072]{1,0:T(8,128)(2,1)} %slice.270), channel_id=1, source_target_pairs={{0,8},{8,0},{16,24},{24,16},{1,9},{9,1},{17,25},{25,17},{2,10},{10... | collective-permute-start | bytes 9437192 | tf_op jit(solution)/shard_map/ppermute | solution.py:162
  80.0 550.1 %all-gather.22.cloned.1.call-start = ((), (), s32[]{:S(2)}) async-start(), calls=%async_computation.11 | async-start | bytes 9437184 | tf_op jit(solution)/shard_map/all_gather | solution.py:290
  173.9 91.8 %collective-permute-start.5 = (bf16[2624,512]{1,0:T(8,128)(2,1)}, bf16[2624,512]{1,0:T(8,128)(2,1)}, u32[]{:S(2)}, u32[]{:S(2)}) collective-permute-start(bf16[2624,512]{1,0:T(8,128)(2,1)} %bitcast.518), channel_id=1, source_target_pairs={{0,8},{8,0},{16,24},{24,16},{1,9},{9,1},{17,25},{25,17},{2,10},{10... | collective-permute-start | bytes 8060936 | tf_op jit(solution)/shard_map/ppermute | solution.py:162
  248.5 147.4 %collective-permute-start.6 = (bf16[512,4096]{1,0:T(8,128)(2,1)}, bf16[512,4096]{1,0:T(8,128)(2,1)}, u32[]{:S(2)}, u32[]{:S(2)}) collective-permute-start(bf16[512,4096]{1,0:T(8,128)(2,1)} %all-gather.20.cloned.1.call-done), channel_id=1, source_target_pairs={{0,8},{8,0},{16,24},{24,16},{1,9},{9,1},{17,25},{25,17},{2,10},{10... | collective-permute-start | bytes 12582920 | tf_op jit(solution)/shard_map/ppermute | solution.py:162
  259.0 101.1 %collective-permute-start.2 = (bf16[256,2048]{1,0:T(8,128)(2,1)S(1)}, bf16[256,2048]{1,0:T(8,128)(2,1)}, u32[]{:S(2)}, u32[]{:S(2)}) collective-permute-start(bf16[256,2048]{1,0:T(8,128)(2,1)S(1)} %pad_maximum_fusion.22), channel_id=1, source_target_pairs={{1,0},{2,1},{3,2},{4,3},{5,4},{6,5},{7,6},{9,8},{10,9},{11,10},{12... | collective-permute-start | bytes 3145736 | tf_op jit(solution)/shard_map/ppermute | solution.py:23
  260.3 99.8 %collective-permute-start.1 = (bf16[256,2048]{1,0:T(8,128)(2,1)S(1)}, bf16[256,2048]{1,0:T(8,128)(2,1)}, u32[]{:S(2)}, u32[]{:S(2)}) collective-permute-start(bf16[256,2048]{1,0:T(8,128)(2,1)S(1)} %pad_maximum_fusion.22), channel_id=1, source_target_pairs={{0,1},{1,2},{2,3},{3,4},{4,5},{5,6},{6,7},{8,9},{9,10},{10,11},{11... | collective-permute-start | bytes 3145736 | tf_op jit(solution)/shard_map/ppermute | solution.py:23
  447.4 535.3 %reduce-scatter.10.cloned.1.call-start = ((), (), s32[]{:S(2)}) async-start(), calls=%async_computation.12 | async-start | bytes 9437184 | tf_op jit(solution)/shard_map/reduce_scatter | solution.py:362
  448.1 66.5 %collective-permute-start.7 = (bf16[512,5248]{1,0:T(8,128)(2,1)}, bf16[512,5248]{1,0:T(8,128)(2,1)}, u32[]{:S(2)}, u32[]{:S(2)}) collective-permute-start(bf16[512,5248]{1,0:T(8,128)(2,1)} %bitcast.494), channel_id=1, source_target_pairs={{0,8},{8,0},{16,24},{24,16},{1,9},{9,1},{17,25},{25,17},{2,10},{10... | collective-permute-start | bytes 16121864 | tf_op jit(solution)/shard_map/ppermute | solution.py:162
  834.9 454.4 %reduce-scatter.18.cloned.1.call-start = ((), (), s32[]{:S(2)}) async-start(), calls=%async_computation.16 | async-start | bytes 589824 | tf_op jit(solution)/shard_map/reduce_scatter | solution.py:209
  880.2 415.3 %reduce-scatter.26.cloned.1.call-start = ((), (), s32[]{:S(2)}) async-start(), calls=%async_computation.22 | async-start | bytes 1511424 | tf_op jit(solution)/shard_map/reduce_scatter | solution.py:223
  885.4 126.6 %collective-permute-start.26 = (bf16[2624,256]{1,0:T(8,128)(2,1)}, bf16[2624,256]{1,0:T(8,128)(2,1)}, u32[]{:S(2)}, u32[]{:S(2)}) collective-permute-start(bf16[2624,256]{1,0:T(8,128)(2,1)} %constant_dynamic-slice_fusion.14), channel_id=1, source_target_pairs={{0,16},{8,24},{16,0},{24,8},{1,17},{9,25},{17,1},{25,9},{2,18},{10... | collective-permute-start | bytes 4030472 | tf_op jit(solution)/shard_map/ppermute | solution.py:162
  896.5 118.4 %collective-permute-start.22 = (bf16[8,32,5248]{2,1,0:T(8,128)(2,1)}, bf16[8,32,5248]{2,1,0:T(8,128)(2,1)}, u32[]{:S(2)}, u32[]{:S(2)}) collective-permute-start(bf16[8,32,5248]{2,1,0:T(8,128)(2,1)} %dynamic-slice_bitcast_fusion.6), channel_id=1, source_target_pairs={{0,16},{8,24},{16,0},{24,8},{1,17},{9,25},{17,1},{25,9},{2,18},{10... | collective-permute-start | bytes 8060936 | tf_op jit(solution)/shard_map/ppermute | solution.py:162
  1014.9 288.9 %reduce-scatter.22.cloned.1.call-start = ((), (), s32[]{:S(2)}) async-start(), calls=%async_computation.19 | async-start | bytes 3022848 | tf_op jit(solution)/shard_map/reduce_scatter | solution.py:209
  1019.8 337.2 %reduce-scatter.20.cloned.1.call-start = ((), (), s32[]{:S(2)}) async-start(), calls=%async_computation.17 | async-start | bytes 3022848 | tf_op jit(solution)/shard_map/reduce_scatter | solution.py:209
  1043.8 62.9 %collective-permute-start.20 = (bf16[8,32,5248]{2,1,0:T(8,128)(2,1)}, bf16[8,32,5248]{2,1,0:T(8,128)(2,1)}, u32[]{:S(2)}, u32[]{:S(2)}) collective-permute-start(bf16[8,32,5248]{2,1,0:T(8,128)(2,1)} %dynamic-slice_bitcast_fusion.7), channel_id=1, source_target_pairs={{0,16},{8,24},{16,0},{24,8},{1,17},{9,25},{17,1},{25,9},{2,18},{10... | collective-permute-start | bytes 8060936 | tf_op jit(solution)/shard_map/ppermute | solution.py:162
  1098.7 56.3 %collective-permute-start.10 = (bf16[256,2048]{0,1:T(8,128)(2,1)}, bf16[256,2048]{0,1:T(8,128)(2,1)S(1)}, u32[]{:S(2)}, u32[]{:S(2)}) collective-permute-start(bf16[256,2048]{0,1:T(8,128)(2,1)} %get-tuple-element.851), channel_id=1, source_target_pairs={{0,1},{1,2},{2,3},{3,4},{4,5},{5,6},{6,7},{8,9},{9,10},{10,11},{11... | collective-permute-start | bytes 3145736 | tf_op jit(solution)/shard_map/ppermute | solution.py:23
  1102.2 52.7 %collective-permute-start.9 = (bf16[256,2048]{0,1:T(8,128)(2,1)}, bf16[256,2048]{0,1:T(8,128)(2,1)}, u32[]{:S(2)}, u32[]{:S(2)}) collective-permute-start(bf16[256,2048]{0,1:T(8,128)(2,1)} %get-tuple-element.850), channel_id=1, source_target_pairs={{1,0},{2,1},{3,2},{4,3},{5,4},{6,5},{7,6},{9,8},{10,9},{11,10},{12... | collective-permute-start | bytes 3145736 | tf_op jit(solution)/shard_map/ppermute | solution.py:23
  1110.7 247.6 %reduce-scatter.16.cloned.1.call-start = ((), (), s32[]{:S(2)}) async-start(), calls=%async_computation.15 | async-start | bytes 589824 | tf_op jit(solution)/shard_map/reduce_scatter | solution.py:209
  1122.3 53.7 %collective-permute-start.13 = (bf16[16,32,3072]{2,1,0:T(8,128)(2,1)}, bf16[16,32,3072]{2,1,0:T(8,128)(2,1)}, u32[]{:S(2)}, u32[]{:S(2)}) collective-permute-start(bf16[16,32,3072]{2,1,0:T(8,128)(2,1)} %dynamic-slice_bitcast_fusion.4), channel_id=1, source_target_pairs={{0,8},{8,0},{16,24},{24,16},{1,9},{9,1},{17,25},{25,17},{2,10},{10... | collective-permute-start | bytes 9437192 | tf_op jit(solution)/shard_map/ppermute | solution.py:162
  1170.1 73.6 %collective-permute-start.11 = (bf16[16,32,3072]{2,1,0:T(8,128)(2,1)}, bf16[16,32,3072]{2,1,0:T(8,128)(2,1)}, u32[]{:S(2)}, u32[]{:S(2)}) collective-permute-start(bf16[16,32,3072]{2,1,0:T(8,128)(2,1)} %dynamic-slice_bitcast_fusion.5), channel_id=1, source_target_pairs={{0,8},{8,0},{16,24},{24,16},{1,9},{9,1},{17,25},{25,17},{2,10},{10... | collective-permute-start | bytes 9437192 | tf_op jit(solution)/shard_map/ppermute | solution.py:162
  1175.9 223.3 %reduce-scatter.24.cloned.1.call-start = ((), (), s32[]{:S(2)}) async-start(), calls=%async_computation.21 | async-start | bytes 1511424 | tf_op jit(solution)/shard_map/reduce_scatter | solution.py:223
  1205.0 262.2 %reduce-scatter.14.cloned.1.call-start = ((), (), s32[]{:S(2)}) async-start(), calls=%async_computation.14 | async-start | bytes 1769472 | tf_op jit(solution)/shard_map/reduce_scatter | solution.py:209
  1243.4 291.4 %reduce-scatter.12.cloned.1.call-start = ((), (), s32[]{:S(2)}) async-start(), calls=%async_computation.13 | async-start | bytes 1769472 | tf_op jit(solution)/shard_map/reduce_scatter | solution.py:209
  1283.8 269.8 %all-gather.26.cloned.1.call-start = ((), (), s32[]{:S(2)}) async-start(), calls=%async_computation.20 | async-start | bytes 1679360 | tf_op jit(solution)/shard_map/all_gather | solution.py:210
  1303.8 269.8 %all-gather.24.cloned.1.call-start = ((), (), s32[]{:S(2)}) async-start(), calls=%async_computation.18 | async-start | bytes 1679360 | tf_op jit(solution)/shard_map/all_gather | solution.py:210
  (155 other events, 4154.8 us)
Sparse Core Ops, SparseCore 0:
  10.8 64.6 all-gather.17
  78.2 38.8 all-gather.27
  119.8 54.1 all-gather.31
  176.5 71.9 all-gather.19
  251.1 108.8 all-gather.29
  362.0 86.0 all-gather.33
  450.3 53.5 all-gather.35
  506.6 123.5 all-gather.21
  835.0 147.5 reduce-scatter.9
  986.2 60.8 reduce-scatter.17
  1050.5 61.0 reduce-scatter.25
  1115.6 81.6 reduce-scatter.21
  1200.9 69.7 reduce-scatter.19
  1273.9 60.9 reduce-scatter.15
  1338.5 60.6 reduce-scatter.23
  1403.4 63.6 reduce-scatter.13
  1471.0 63.7 reduce-scatter.11
  1536.3 17.2 all-gather.25
  1555.2 18.3 all-gather.23

commit v2 on v1

--- a/solution.py
+++ b/solution.py
@@ -174,22 +174,31 @@
     return (jnp.where(flag == 0, own, other), jnp.where(flag == 0, other, own))
 
 
-def gather_rows(shard, core):
+def after(value, anchor):
+    return lax.optimization_barrier((value, anchor))[0]
+
+
+def begin_rows(shard, core):
     half = shard.shape[0] // 2
-    own = lax.all_gather(
+    return lax.all_gather(
         lax.dynamic_slice_in_dim(shard, core * half, half, 0), "fsdp", axis=0, tiled=True
     )
-    low, high = ordered(core, own, swap_core(own))
-    width = shard.shape[1]
-    pair = [part.reshape(-1, 1, half, width) for part in (low, high)]
+
+
+def end_rows(own, core):
+    half, width = own.shape[0] // lax.axis_size("fsdp"), own.shape[1]
+    pair = [part.reshape(-1, 1, half, width) for part in ordered(core, own, swap_core(own))]
     return jnp.concatenate(pair, axis=1).reshape(-1, width)
 
 
-def gather_columns(shard, core):
+def begin_columns(shard, core):
     half = shard.shape[1] // 2
-    own = lax.all_gather(
+    return lax.all_gather(
         lax.dynamic_slice_in_dim(shard, core * half, half, 1), "fsdp", axis=0, tiled=True
     )
+
+
+def end_columns(own, core):
     return jnp.concatenate(ordered(core, own, swap_core(own)), axis=1)
 
 
@@ -199,15 +208,13 @@
     return (kept.astype(jnp.float32) + exchange(sent).astype(jnp.float32)).astype(jnp.bfloat16)
 
 
-def reduce_rows(gradient, core, plane):
+def quarter_rows(gradient, core, plane):
     count = lax.axis_size("fsdp")
     rows, width = gradient.shape
     piece = rows // count // 4
     parts = gradient.astype(jnp.bfloat16).reshape(count * 2, 2, piece, width)
     parts = halve(parts, core, swap_core).reshape(count, 2, piece, width)
-    parts = halve(parts, plane, swap_plane).reshape(count * piece, width)
-    own = lax.psum_scatter(parts, "fsdp", scatter_dimension=0, tiled=True)
-    return lax.all_gather(own, "rep", axis=0, tiled=True).astype(jnp.float32)
+    return halve(parts, plane, swap_plane)
 
 
 def halve_columns(value, flag, exchange):
@@ -217,12 +224,36 @@
     return (kept.astype(jnp.float32) + exchange(sent).astype(jnp.float32)).astype(jnp.bfloat16)
 
 
-def reduce_columns(gradient, core, plane):
+def quarter_columns(gradient, core, plane, piece):
     parts = halve_columns(gradient.astype(jnp.bfloat16), core, swap_core)
     parts = halve_columns(parts, plane, swap_plane)
-    own = lax.psum_scatter(parts, "fsdp", scatter_dimension=0, tiled=True)
+    return parts.reshape(lax.axis_size("fsdp"), piece, -1)
+
+
+def scatter_shares(blocks):
+    count, piece = blocks[0].shape[:2]
+    joined = jnp.concatenate(blocks, axis=2).reshape(count * piece, -1)
+    own = lax.psum_scatter(joined, "fsdp", scatter_dimension=0, tiled=True)
     every = lax.all_gather(own, "rep", axis=0, tiled=False)
+    shares, start = [], 0
+    for block in blocks:
+        shares.append(every[:, :, start : start + block.shape[2]])
+        start += block.shape[2]
+    return shares
+
+
+def whole_rows(share):
+    return share.reshape(-1, share.shape[2]).astype(jnp.float32)
+
+
+def whole_columns(share):
+    every = share.reshape(4, -1, D // 4)
     return jnp.concatenate([every[0], every[2], every[1], every[3]], axis=1).astype(jnp.float32)
+
+
+def gain_block(rows, piece):
+    split = rows.astype(jnp.bfloat16).reshape(rows.shape[0], lax.axis_size("fsdp"), -1)
+    return jnp.pad(jnp.transpose(split, (1, 0, 2)), ((0, 0), (0, piece - rows.shape[0]), (0, 0)))
 
 
 def on_device(
@@ -237,19 +268,22 @@
     shard_rows = attn_gain.shape[1]
     half_rows = shard_rows // 2
 
-    gains = jnp.concatenate([attn_gain, mlp_gain], axis=0)
-    first = lax.dynamic_slice_in_dim(w_qkv[0], core * half_rows, half_rows, 0)
-    gain_block = jnp.pad(gains, ((0, half_rows - 2 * LAYERS), (0, 0)))
+    marks = jnp.stack([segment_ids, positions // 64, positions % 64]).astype(jnp.bfloat16)
+    gains = jnp.concatenate([attn_gain, mlp_gain, marks.reshape(-1, shard_rows)], axis=0)
+    first = jnp.concatenate([w_qkv[0], w_out[0]], axis=1)
+    first = lax.dynamic_slice_in_dim(first, core * half_rows, half_rows, 0)
+    spare = jnp.pad(gains, ((0, half_rows - gains.shape[0]), (0, 0)))
     own = lax.all_gather(
-        jnp.concatenate([first, gain_block], axis=1), "fsdp", axis=0, tiled=True
-    )
-    low, high = ordered(core, own[:, : 3 * D], swap_core(own[:, : 3 * D]))
-    pair = [part.reshape(-1, 1, half_rows, 3 * D) for part in (low, high)]
-    qkv_first = jnp.concatenate(pair, axis=1).reshape(D, 3 * D)
-    all_gains = own[:, 3 * D :].reshape(-1, half_rows, shard_rows)[:, : 2 * LAYERS]
-    all_gains = jnp.transpose(all_gains, (1, 0, 2)).reshape(2 * LAYERS, D).astype(jnp.float32)
-
-    marks = lax.all_gather(jnp.stack([segment_ids, positions]), "fsdp", axis=1, tiled=True)
+        jnp.concatenate([first, spare], axis=1), "fsdp", axis=0, tiled=True
+    )
+    both_first = end_rows(own[:, : 4 * D], core)
+    small = own[:, 4 * D :].reshape(-1, half_rows, shard_rows)
+    all_gains = jnp.transpose(small[:, : 2 * LAYERS], (1, 0, 2))
+    all_gains = all_gains.reshape(2 * LAYERS, D).astype(jnp.float32)
+    marks = small[:, 2 * LAYERS : gains.shape[0]].reshape(-1, 3, row_count)
+    marks = jnp.transpose(marks, (1, 0, 2)).reshape(3, -1).astype(jnp.int32)
+    marks = jnp.stack([marks[0], marks[1] * 64 + marks[2]])
+
     padded = jnp.pad(marks, ((0, 0), (hops * row_count, hops * row_count)), constant_values=-1)
     near = lax.dynamic_slice_in_dim(padded, place * row_count, len(offsets) * row_count, 1)
     allowed_near = (segment_ids[:, None] == near[0][None, :]) & (
@@ -257,20 +291,22 @@
     )
     allowed_all = segment_ids[:, None] == marks[0][None, :]
 
-    out_first = gather_rows(w_out[0], core)
-    in_first = gather_rows(w_in[0], core)
-    down_first = gather_columns(w_down[0], core)
-    both = gather_rows(jnp.concatenate([w_qkv[1], w_out[1]], axis=1), core)
-    matrices = (
-        (qkv_first, out_first, in_first, down_first),
-        (both[:, : 3 * D], both[:, 3 * D :], gather_rows(w_in[1], core), gather_columns(w_down[1], core)),
-    )
+    began = (
+        (None, begin_rows(w_in[0], core), begin_columns(w_down[0], core)),
+        (
+            begin_rows(jnp.concatenate([w_qkv[1], w_out[1]], axis=1), core),
+            begin_rows(w_in[1], core),
+            begin_columns(w_down[1], core),
+        ),
+    )
+    matrices = []
+    both = both_first
 
     hidden = tokens.astype(jnp.float32)
     memory = []
     for layer_index in range(LAYERS):
         base_theta = LOCAL_THETA if layer_index == 0 else GLOBAL_THETA
-        mat_qkv, mat_out, mat_in, mat_down = matrices[layer_index]
+        mat_qkv, mat_out = (both[:, : 3 * D], both[:, 3 * D :])
         normed = layer_norm(hidden, all_gains[layer_index]).astype(jnp.bfloat16)
         projected = jnp.dot(normed, mat_qkv, preferred_element_type=jnp.float32)
         queries = rotate(projected[:, :D], positions, base_theta).astype(jnp.bfloat16)
@@ -292,10 +328,15 @@
         key_rows, value_rows = (rows[:, :D], rows[:, D:])
         attended, log_sums = attend_forward(queries, key_rows, value_rows, allowed)
         attended = attended.astype(jnp.bfloat16)
+        mat_in = end_rows(after(began[layer_index][1], attended), core)
         middle = hidden + jnp.dot(attended, mat_out, preferred_element_type=jnp.float32)
         normed_mlp = layer_norm(middle, all_gains[LAYERS + layer_index]).astype(jnp.bfloat16)
+        mat_down = end_columns(after(began[layer_index][2], normed_mlp), core)
         raised = jnp.dot(normed_mlp, mat_in, preferred_element_type=jnp.float32)
         gated_hidden = gelu_gate(raised).astype(jnp.bfloat16)
+        if layer_index + 1 < LAYERS:
+            both = end_rows(after(began[layer_index + 1][0], gated_hidden), core)
+        matrices.append((mat_qkv, mat_out, mat_in, mat_down))
         output = middle + jnp.dot(gated_hidden, mat_down, preferred_element_type=jnp.float32)
         memory.append(
             (
@@ -335,17 +376,19 @@
         ) = memory[layer_index]
         mat_qkv, mat_out, mat_in, mat_down = matrices[layer_index]
         grad_branch = grad_hidden.astype(jnp.bfloat16)
-        own_down = reduce_columns(contract_rows(gated_hidden, grad_branch), core, plane)
+        own_down = quarter_columns(
+            contract_rows(gated_hidden, grad_branch), core, plane, shard_rows // 4
+        )
         grad_gated = contract_cols(grad_branch, mat_down)
         unused, pull_gate = jax.vjp(gelu_gate, raised)
         grad_raised = pull_gate(grad_gated)[0].astype(jnp.bfloat16)
-        own_in = reduce_rows(contract_rows(normed_mlp, grad_raised), core, plane)
+        own_in = quarter_rows(contract_rows(normed_mlp, grad_raised), core, plane)
         grad_normed_mlp = contract_cols(grad_raised, mat_in)
         unused, pull_norm = jax.vjp(layer_norm, middle, all_gains[LAYERS + layer_index])
         grad_middle_part, gain_rows[LAYERS + layer_index] = pull_norm(grad_normed_mlp)
         grad_middle = grad_hidden + grad_middle_part
         grad_attn_in = grad_middle.astype(jnp.bfloat16)
-        own_out = reduce_rows(contract_rows(attended, grad_attn_in), core, plane)
+        own_out = quarter_rows(contract_rows(attended, grad_attn_in), core, plane)
         grad_mixed = contract_cols(grad_attn_in, mat_out).astype(jnp.bfloat16)
         grad_queries, grad_keys, grad_values, inner = attend_backward(
             queries, key_rows, value_rows, grad_mixed, log_sums, allowed
@@ -361,7 +404,8 @@
         else:
             summed = lax.psum_scatter(
                 pair_grads.astype(jnp.bfloat16), "fsdp", scatter_dimension=0, tiled=True
-            ).astype(jnp.float32)
+            )
+            summed = after(summed, (own_down, own_in, own_out)).astype(jnp.float32)
         grad_projected = jnp.concatenate(
             [
                 rotate_back(grad_queries, positions, base_theta),
@@ -370,22 +414,34 @@
             ],
             axis=1,
         ).astype(jnp.bfloat16)
-        own_qkv = reduce_rows(contract_rows(normed, grad_projected), core, plane)
+        own_qkv = quarter_rows(contract_rows(normed, grad_projected), core, plane)
         grad_normed = contract_cols(grad_projected, mat_qkv)
         unused, pull_first = jax.vjp(layer_norm, layer_input, all_gains[layer_index])
         grad_hidden_part, gain_rows[layer_index] = pull_first(grad_normed)
         grad_hidden = grad_middle + grad_hidden_part
-        owned[layer_index] = (own_qkv, own_out, own_in, own_down)
-    gain_sums = lax.psum(jnp.stack(gain_rows), ("rep", "fsdp"))
-    gain_own = lax.dynamic_slice_in_dim(gain_sums, place * shard_rows, shard_rows, 1)
-    grads = [jnp.stack([owned[0][index], owned[1][index]]) for index in range(4)]
+        gain_part = gain_block(
+            jnp.stack([gain_rows[layer_index], gain_rows[LAYERS + layer_index]]), shard_rows // 4
+        )
+        if layer_index == 0:
+            wide = scatter_shares([own_down, own_in, own_out])
+            wide = wide + scatter_shares([own_qkv, gain_part])
+        else:
+            wide = scatter_shares([own_down, own_in, own_out, own_qkv, gain_part])
+        owned[layer_index] = (
+            whole_rows(wide[3]),
+            whole_rows(wide[2]),
+            whole_rows(wide[1]),
+            whole_columns(wide[0]),
+            jnp.sum(wide[4][:, :2].astype(jnp.float32), axis=0),
+        )
+    grads = [jnp.stack([owned[0][index], owned[1][index]]) for index in range(5)]
     return (
         hidden.astype(jnp.bfloat16),
         grad_hidden,
-        gain_own[:LAYERS],
+        grads[4][:, 0],
         grads[0],
         grads[1],
-        gain_own[LAYERS:],
+        grads[4][:, 1],
         grads[2],
         grads[3],
     )

time: 1590 us -> 1570 us (0.987)
  blocking collectives: 116 us -> 9.17 us
  local copies, waits for them, and re-layouts: 172 us -> 217 us
  waiting for transfers between devices: 847 us -> 890 us
    ppermute x23 -> x22, waiting for transfers between devices: 118 us -> 267 us  [swap(): lax.ppermute(value, 'rep', [(source, source ^ bit) for source in range(co...]
    reduce_scatter x8 -> x3, waiting for transfers between devices: 149 us -> 59.5 us  [scatter_shares(): own = lax.psum_scatter(joined, 'fsdp', scatter_dimension=0, tiled=True)]
    ppermute x4, waiting for transfers between devices: 32.2 us -> 118 us  [shifted(): lax.ppermute(value, axis, [(source, source + steps) for source in range(f...]
    all_gather x9 -> x8, waiting for transfers between devices: 365 us -> 283 us  [the longest x2 96.6 us: begin_columns(): lax.all_gather(lax.dynamic_slice_in_dim(shard, core * half, half, 1), 'fs...]
    all_gather x7 -> x1, blocking collectives: 73.8 us -> 9.17 us  [scatter_shares(): every = lax.all_gather(own, 'rep', axis=0, tiled=False)]
    reduce_scatter x1, waiting for transfers between devices: 85.5 us -> 41.1 us  [on_device(): lax.psum_scatter(pair_grads.astype(jnp.bfloat16), 'fsdp', scatter_dimensi...]
    psum x1 -> x0, blocking collectives: 42 us -> none  [on_device(): gain_sums = lax.psum(jnp.stack(gain_rows), ('rep', 'fsdp'))]
    concatenate x0 -> x12, local copies, waits for them, and re-layouts: none -> 41.4 us  [the longest x4 30.1 us: scatter_shares(): joined = jnp.concatenate(blocks, axis=2).reshape(count * piece, -1)]
  transfers between devices with their start and end apart: 46 -> 39, of which waited for: 23 -> 26; matrix products, arithmetic and copies ran while one was open for 21% -> 22% of each run, Pallas kernels for 0% -> 0%
where the time goes in v2:
time: 1570 us; the launch traced here: 1560 us
  waiting for transfers between devices  890 us (57%)
  local copies, waits for them, and re-layouts  217 us (14%)
  matrix products  198 us (13%)
  other arithmetic  193 us (12%)
  starting transfers between devices  23.2 us (1%)
  between operations  16.3 us (1%)
    ppermute x22, waiting for transfers between devices, swap(): lax.ppermute(value, 'rep', [(source, source ^ bit) for source in range(co...  267 us
    all_gather x1, waiting for transfers between devices, on_device(): rows = lax.all_gather(pairs, 'fsdp', axis=0, tiled=True)  120 us
    ppermute x4, waiting for transfers between devices, shifted(): lax.ppermute(value, axis, [(source, source + steps) for source in range(f...  118 us
    all_gather x2, waiting for transfers between devices, begin_columns(): lax.all_gather(lax.dynamic_slice_in_dim(shard, core * half, half, 1), 'fs...  96.6 us
    all_gather x1, waiting for transfers between devices, on_device(): lax.all_gather(jnp.concatenate([first, spare], axis=1), 'fsdp', axis=0, t...  75.5 us
    all_gather x3, waiting for transfers between devices, begin_rows(): lax.all_gather(lax.dynamic_slice_in_dim(shard, core * half, half, 0), 'fs...  74.5 us
    reduce_scatter x3, waiting for transfers between devices, scatter_shares(): own = lax.psum_scatter(joined, 'fsdp', scatter_dimension=0, tiled=True)  59.5 us
    dot_general x8, matrix products, contract_cols(): lax.dot_general(left, right, (((1,), (1,)), ((), ())), preferred_element_...  46.4 us
  transfers between devices with their start and end apart: 39, of which 26 were waited for; matrix products, arithmetic and copies ran while one was open for 22% of the time, Pallas kernels for 0%

profile of v2, /device:TPU:0, one launch (start us, length us, event | category | flops | bytes accessed | tf_op | source)
XLA Modules:
  0.0 1558.4 jit_solution(9042071157593974297)
XLA Ops:
  16.3 75.5 %all-gather.17.cloned.1.call-done = bf16[512,4224]{1,0:T(8,128)(2,1)} async-done(((bf16[64,4224]{1,0:T(8,128)(2,1)}), bf16[512,4224]{1,0:T(8,128)(2,1)}) %all-gather.17.cloned.1.call-update) | async-done | bytes 4325392 | tf_op jit(solution)/shard_map/all_gather | solution.py:276
  138.7 34.7 %collective-permute-done.2 = bf16[256,2048]{1,0:T(8,128)(2,1)} collective-permute-done((bf16[256,2048]{1,0:T(8,128)(2,1)}, bf16[256,2048]{1,0:T(8,128)(2,1)}, u32[]{:S(2)}, u32[]{:S(2)}) %collective-permute-start.2) | collective-permute-done | bytes 1048608 | tf_op jit(solution)/shard_map/ppermute | solution.py:23
  173.4 23.7 %collective-permute-done.1 = bf16[256,2048]{1,0:T(8,128)(2,1)} collective-permute-done((bf16[256,2048]{1,0:T(8,128)(2,1)}, bf16[256,2048]{1,0:T(8,128)(2,1)}, u32[]{:S(2)}, u32[]{:S(2)}) %collective-permute-start.1) | collective-permute-done | bytes 1048608 | tf_op jit(solution)/shard_map/ppermute | solution.py:23
  203.1 24.5 %while.64 = (s32[]{:T(128)}, bf16[4,256,256]{1,2,0:T(8,128)(2,1)}, f32[4,4,256]{2,1,0:T(4,128)S(1)}, s32[4]{0:T(128)S(1)}, bf16[768,1024]{0,1:T(8,128)(2,1)S(1)}...) while((s32[]{:T(128)}, bf16[4,256,256]{1,2,0:T(8,128)(2,1)}, ...), condition=%wide.region_5.6_spmd.clone, body=%wide.region_2.5_spmd.clone.sunk | while | flops 211745792 | bytes 13410527 | solution.py:109
  234.2 45.3 %all-gather.25.cloned.1.call-done = bf16[1,2624,512]{2,1,0:T(8,128)(2,1)} async-done(((bf16[1,328,512]{2,1,0:T(8,128)(2,1)}), bf16[1,2624,512]{2,1,0:T(8,128)(2,1)}) %all-gather.25.cloned.1.call-update) | async-done | bytes 2686992 | tf_op jit(solution)/shard_map/all_gather | solution.py:196
  279.5 9.2 broadcast_select_fusion.3
  307.9 46.2 %all-gather.19.cloned.1.call-done = bf16[512,4096]{1,0:T(8,128)(2,1)} async-done(((bf16[64,4096]{1,0:T(8,128)(2,1)}), bf16[512,4096]{1,0:T(8,128)(2,1)}) %all-gather.19.cloned.1.call-update) | async-done | bytes 4194320 | tf_op jit(solution)/shard_map/all_gather | solution.py:183
  388.2 120.3 %all-gather.21.cloned.1.call-done = bf16[2048,2048]{1,0:T(8,128)(2,1)} async-done(((bf16[256,2048]{1,0:T(8,128)(2,1)}), bf16[2048,2048]{1,0:T(8,128)(2,1)}) %all-gather.21.cloned.1.call-update) | async-done | bytes 8388624 | tf_op jit(solution)/shard_map/all_gather | solution.py:326
  528.1 40.8 %while.65 = (s32[]{:T(128)}, bf16[4,256,256]{1,2,0:T(8,128)(2,1)S(1)}, f32[4,4,256]{2,1,0:T(4,128)S(1)}, s32[4]{0:T(128)S(1)}, bf16[2048,1024]{0,1:T(8,128)(2,1)...) while((s32[]{:T(128)}, ...), condition=%wide.region_13.14_spmd.clone, body=%wide.region_10.13_spmd.clone.sunk | while | flops 562560000 | bytes 34383056 | solution.py:109
  568.9 28.4 %all-gather.27.cloned.1.call-done = bf16[1,512,5248]{2,1,0:T(8,128)(2,1)} async-done(((bf16[1,64,5248]{2,1,0:T(8,128)(2,1)}), bf16[1,512,5248]{2,1,0:T(8,128)(2,1)}) %all-gather.27.cloned.1.call-update) | async-done | bytes 5373968 | tf_op jit(solution)/shard_map/all_gather | solution.py:183
  601.7 51.3 %all-gather.29.cloned.1.call-done = bf16[1,2624,512]{2,1,0:T(8,128)(2,1)} async-done(((bf16[1,328,512]{2,1,0:T(8,128)(2,1)}), bf16[1,2624,512]{2,1,0:T(8,128)(2,1)}) %all-gather.29.cloned.1.call-update) | async-done | bytes 2686992 | tf_op jit(solution)/shard_map/all_gather | solution.py:196
  663.6 9.2 broadcast_select_fusion.1
  681.7 9.7 fusion.103
  694.9 7.7 multiply_reduce_fusion.2
  710.0 101.9 %while.66 = (s32[]{:T(128)}, f32[4,256,256]{1,2,0:T(8,128)}, bf16[4,2048,256]{1,2,0:T(8,128)(2,1)}, bf16[4,2048,256]{1,2,0:T(8,128)(2,1)}, s32[4]{0:T(128)S(1)},...) while((s32[]{:T(128)}, f32[4,256,256]{1,2,0:T(8,128)}, ...), condition=%wide.region_20.21_spmd.clone, body=%wide.region_18.20_spmd.clone.sunk | while | flops 1375271936 | bytes 105944344 | solution.py:156
  811.9 8.5 pad_maximum_fusion.4
  833.8 9.0 collective-permute-done.8
  856.3 65.4 %collective-permute-done.11 = bf16[8,32,1024]{2,1,0:T(8,128)(2,1)S(1)} collective-permute-done((bf16[8,32,1024]{2,1,0:T(8,128)(2,1)S(1)}, bf16[8,32,1024]{2,1,0:T(8,128)(2,1)S(1)}, u32[]{:S(2)}, u32[]{:S(2)}) %collective-permute-start.11) | collective-permute-done | bytes 524320 | tf_op jit(solution)/shard_map/ppermute | solution.py:162
  927.4 41.1 %reduce-scatter.5.cloned.1.call-done = bf16[256,2048]{0,1:T(8,128)(2,1)} async-done(((bf16[2048,2048]{0,1:T(8,128)(2,1)}), bf16[256,2048]{0,1:T(8,128)(2,1)}) %reduce-scatter.5.cloned.1.call-update) | async-done | bytes 1048592 | tf_op jit(solution)/shard_map/reduce_scatter | solution.py:405
  1002.2 9.9 multiply_reduce_fusion.4
  1035.9 90.3 %collective-permute-done.25 = bf16[8,32,1024]{2,1,0:T(8,128)(2,1)S(1)} collective-permute-done((bf16[8,32,1024]{2,1,0:T(8,128)(2,1)S(1)}, bf16[8,32,1024]{2,1,0:T(8,128)(2,1)S(1)}, u32[]{:S(2)}, u32[]{:S(2)}) %collective-permute-start.25) | collective-permute-done | bytes 524320 | tf_op jit(solution)/shard_map/ppermute | solution.py:162
  1137.9 9.4 concatenate.168
  1165.2 26.6 %collective-permute-done.17 = bf16[2624,256]{1,0:T(8,128)(2,1)} collective-permute-done((bf16[2624,256]{1,0:T(8,128)(2,1)}, bf16[2624,256]{1,0:T(8,128)(2,1)}, u32[]{:S(2)}, u32[]{:S(2)}) %collective-permute-start.17) | collective-permute-done | bytes 1343520 | tf_op jit(solution)/shard_map/ppermute | solution.py:162
  1202.6 22.1 %collective-permute-done.19 = bf16[8,32,3072]{2,1,0:T(8,128)(2,1)} collective-permute-done((bf16[8,32,3072]{2,1,0:T(8,128)(2,1)}, bf16[8,32,3072]{2,1,0:T(8,128)(2,1)}, u32[]{:S(2)}, u32[]{:S(2)}) %collective-permute-start.19) | collective-permute-done | bytes 1572896 | tf_op jit(solution)/shard_map/ppermute | solution.py:162
  1227.9 13.0 concatenate.164
  1241.6 44.9 %while.67 = (s32[]{:T(128)}, f32[4,256,256]{1,2,0:T(8,128)S(1)}, f32[4,768,256]{1,2,0:T(8,128)}, f32[4,768,256]{1,2,0:T(8,128)}, s32[4]{0:T(128)S(1)}, /*index=5...) while((s32[]{:T(128)}, f32[4,256,256]{1,2,0:T(8,128)S(1)}, ...), condition=%wide.region_28.29_spmd.clone, body=%wide.region_26.28_spmd.clone.sunk | while | flops 511638528 | bytes 33583360 | solution.py:156
  1295.2 59.5 %collective-permute-done.13 = bf16[256,2048]{0,1:T(8,128)(2,1)S(1)} collective-permute-done((bf16[256,2048]{0,1:T(8,128)(2,1)S(1)}, bf16[256,2048]{0,1:T(8,128)(2,1)S(1)}, u32[]{:S(2)}, u32[]{:S(2)}) %collective-permute-start.13) | collective-permute-done | bytes 1048608 | tf_op jit(solution)/shard_map/ppermute | solution.py:23
  1370.8 32.1 %collective-permute-done.15 = bf16[8,32,3072]{2,1,0:T(8,128)(2,1)S(1)} collective-permute-done((bf16[8,32,3072]{2,1,0:T(8,128)(2,1)S(1)}, bf16[8,32,3072]{2,1,0:T(8,128)(2,1)S(1)}, u32[]{:S(2)}, u32[]{:S(2)}) %collective-permute-start.15) | collective-permute-done | bytes 1572896 | tf_op jit(solution)/shard_map/ppermute | solution.py:162
  1412.7 59.4 %reduce-scatter.7.cloned.1.call-done = bf16[32,3200]{1,0:T(8,128)(2,1)} async-done(((bf16[256,3200]{1,0:T(8,128)(2,1)}), bf16[32,3200]{1,0:T(8,128)(2,1)}) %reduce-scatter.7.cloned.1.call-update) | async-done | bytes 204816 | tf_op jit(solution)/shard_map/reduce_scatter | solution.py:236
  1472.1 9.2 all-gather.4
  1481.4 14.8 all-gather.33.cloned.1.call-done
  1504.8 21.3 %all-gather.31.cloned.1.call-done = bf16[128,12096]{1,0:T(8,128)(2,1)} async-done(((bf16[32,12096]{1,0:T(8,128)(2,1)}), bf16[128,12096]{1,0:T(8,128)(2,1)}) %all-gather.31.cloned.1.call-update) | async-done | bytes 3096592 | tf_op jit(solution)/shard_map/all_gather | solution.py:237
  (762 shorter events, 578.1 us)
Async XLA Ops:
  7.2 84.7 %all-gather.17.cloned.1.call-start = ((), (), s32[]{:S(2)}) async-start(), calls=%async_computation.4 | async-start | bytes 4866048 | tf_op jit(solution)/shard_map/all_gather | solution.py:276
  14.0 213.6 %all-gather.23.cloned.1.call-start = ((), (), s32[]{:S(2)}) async-start(), calls=%async_computation.11 | async-start | bytes 6045696 | tf_op jit(solution)/shard_map/all_gather | solution.py:183
  16.3 263.3 %all-gather.25.cloned.1.call-start = ((), (), s32[]{:S(2)}) async-start(), calls=%async_computation.12 | async-start | bytes 3022848 | tf_op jit(solution)/shard_map/all_gather | solution.py:196
  125.7 47.6 %collective-permute-start.2 = (bf16[256,2048]{1,0:T(8,128)(2,1)}, bf16[256,2048]{1,0:T(8,128)(2,1)}, u32[]{:S(2)}, u32[]{:S(2)}) collective-permute-start(bf16[256,2048]{1,0:T(8,128)(2,1)} %pad_maximum_fusion.21), channel_id=1, source_target_pairs={{1,0},{2,1},{3,2},{4,3},{5,4},{6,5},{7,6},{9,8},{10,9},{11,10},{12... | collective-permute-start | bytes 3145736 | tf_op jit(solution)/shard_map/ppermute | solution.py:23
  127.0 70.0 %collective-permute-start.1 = (bf16[256,2048]{1,0:T(8,128)(2,1)}, bf16[256,2048]{1,0:T(8,128)(2,1)}, u32[]{:S(2)}, u32[]{:S(2)}) collective-permute-start(bf16[256,2048]{1,0:T(8,128)(2,1)} %pad_maximum_fusion.21), channel_id=1, source_target_pairs={{0,1},{1,2},{2,3},{3,4},{4,5},{5,6},{6,7},{8,9},{9,10},{10,11},{11... | collective-permute-start | bytes 3145736 | tf_op jit(solution)/shard_map/ppermute | solution.py:23
  134.3 219.8 %all-gather.19.cloned.1.call-start = ((), (), s32[]{:S(2)}) async-start(), calls=%async_computation.5 | async-start | bytes 4718592 | tf_op jit(solution)/shard_map/all_gather | solution.py:183
  227.6 51.9 %collective-permute-start.3 = (bf16[512,5248]{1,0:T(8,128)(2,1)}, bf16[512,5248]{1,0:T(8,128)(2,1)}, u32[]{:S(2)}, u32[]{:S(2)}) collective-permute-start(bf16[512,5248]{1,0:T(8,128)(2,1)} %bitcast.474), channel_id=1, source_target_pairs={{0,8},{8,0},{16,24},{24,16},{1,9},{9,1},{17,25},{25,17},{2,10},{10... | collective-permute-start | bytes 16121864 | tf_op jit(solution)/shard_map/ppermute | solution.py:162
  229.9 278.6 %all-gather.21.cloned.1.call-start = ((), (), s32[]{:S(2)}) async-start(), calls=%async_computation.6 | async-start | bytes 9437184 | tf_op jit(solution)/shard_map/all_gather | solution.py:326
  279.5 74.6 %collective-permute-start.4 = (bf16[2624,512]{1,0:T(8,128)(2,1)}, bf16[2624,512]{1,0:T(8,128)(2,1)}, u32[]{:S(2)}, u32[]{:S(2)}) collective-permute-start(bf16[2624,512]{1,0:T(8,128)(2,1)} %bitcast.506), channel_id=1, source_target_pairs={{0,8},{8,0},{16,24},{24,16},{1,9},{9,1},{17,25},{25,17},{2,10},{10... | collective-permute-start | bytes 8060936 | tf_op jit(solution)/shard_map/ppermute | solution.py:162
  385.1 212.2 %all-gather.27.cloned.1.call-start = ((), (), s32[]{:S(2)}) async-start(), calls=%async_computation.13 | async-start | bytes 6045696 | tf_op jit(solution)/shard_map/all_gather | solution.py:183
  386.1 266.9 %all-gather.29.cloned.1.call-start = ((), (), s32[]{:S(2)}) async-start(), calls=%async_computation.14 | async-start | bytes 3022848 | tf_op jit(solution)/shard_map/all_gather | solution.py:196
  387.1 581.5 %reduce-scatter.5.cloned.1.call-start = ((), (), s32[]{:S(2)}) async-start(), calls=%async_computation.7 | async-start | bytes 9437184 | tf_op jit(solution)/shard_map/reduce_scatter | solution.py:405
  597.3 66.3 %collective-permute-start.6 = (bf16[512,5248]{1,0:T(8,128)(2,1)}, bf16[512,5248]{1,0:T(8,128)(2,1)}, u32[]{:S(2)}, u32[]{:S(2)}) collective-permute-start(bf16[512,5248]{1,0:T(8,128)(2,1)} %bitcast.476), channel_id=1, source_target_pairs={{0,8},{8,0},{16,24},{24,16},{1,9},{9,1},{17,25},{25,17},{2,10},{10... | collective-permute-start | bytes 16121864 | tf_op jit(solution)/shard_map/ppermute | solution.py:162
  820.4 584.4 %reduce-scatter.11.cloned.1.call-start = ((), (), s32[]{:S(2)}) async-start(), calls=%async_computation.10 | async-start | bytes 5160960 | tf_op jit(solution)/shard_map/reduce_scatter | solution.py:236
  833.6 9.2 collective-permute-start.8
  850.0 72.8 %collective-permute-start.9 = (bf16[8,32,5248]{2,1,0:T(8,128)(2,1)}, bf16[8,32,5248]{2,1,0:T(8,128)(2,1)}, u32[]{:S(2)}, u32[]{:S(2)}) collective-permute-start(bf16[8,32,5248]{2,1,0:T(8,128)(2,1)} %dynamic-slice_bitcast_fusion.7), channel_id=1, source_target_pairs={{0,16},{8,24},{16,0},{24,8},{1,17},{9,25},{17,1},{25,9},{2,18},{10... | collective-permute-start | bytes 8060936 | tf_op jit(solution)/shard_map/ppermute | solution.py:162
  855.5 66.3 %collective-permute-start.11 = (bf16[8,32,1024]{2,1,0:T(8,128)(2,1)S(1)}, bf16[8,32,1024]{2,1,0:T(8,128)(2,1)S(1)}, u32[]{:S(2)}, u32[]{:S(2)}) collective-permute-start(bf16[8,32,1024]{2,1,0:T(8,128)(2,1)S(1)} %dynamic-slice_bitcast_fusion.13), channel_id=1, source_target_pairs={{0,16},{8,24},{16,0},{24,8},{1,17},{9,25},{17,1},{25,9},{2,18},{10... | collective-permute-start | bytes 1572872 | tf_op jit(solution)/shard_map/ppermute | solution.py:162
  995.5 20.6 %collective-permute-start.22 = (bf16[16,32,5248]{2,1,0:T(8,128)(2,1)}, bf16[16,32,5248]{2,1,0:T(8,128)(2,1)}, u32[]{:S(2)}, u32[]{:S(2)}) collective-permute-start(bf16[16,32,5248]{2,1,0:T(8,128)(2,1)} %dynamic-slice_bitcast_fusion.2), channel_id=1, source_target_pairs={{0,8},{8,0},{16,24},{24,16},{1,9},{9,1},{17,25},{25,17},{2,10},{10... | collective-permute-start | bytes 16121864 | tf_op jit(solution)/shard_map/ppermute | solution.py:162
  1001.6 25.6 %collective-permute-start.20 = (bf16[2624,512]{1,0:T(8,128)(2,1)}, bf16[2624,512]{1,0:T(8,128)(2,1)}, u32[]{:S(2)}, u32[]{:S(2)}) collective-permute-start(bf16[2624,512]{1,0:T(8,128)(2,1)} %constant_dynamic-slice_fusion.15), channel_id=1, source_target_pairs={{0,8},{8,0},{16,24},{24,16},{1,9},{9,1},{17,25},{25,17},{2,10},{10... | collective-permute-start | bytes 8060936 | tf_op jit(solution)/shard_map/ppermute | solution.py:162
  1015.1 17.5 %collective-permute-start.24 = (bf16[16,32,1024]{2,1,0:T(8,128)(2,1)S(1)}, bf16[16,32,1024]{2,1,0:T(8,128)(2,1)}, u32[]{:S(2)}, u32[]{:S(2)}) collective-permute-start(bf16[16,32,1024]{2,1,0:T(8,128)(2,1)S(1)} %dynamic-slice_bitcast_fusion.10), channel_id=1, source_target_pairs={{0,8},{8,0},{16,24},{24,16},{1,9},{9,1},{17,25},{25,17},{2,10},{10... | collective-permute-start | bytes 3145736 | tf_op jit(solution)/shard_map/ppermute | solution.py:162
  1025.7 107.4 %collective-permute-start.23 = (bf16[8,32,5248]{2,1,0:T(8,128)(2,1)}, bf16[8,32,5248]{2,1,0:T(8,128)(2,1)}, u32[]{:S(2)}, u32[]{:S(2)}) collective-permute-start(bf16[8,32,5248]{2,1,0:T(8,128)(2,1)} %dynamic-slice_bitcast_fusion.6), channel_id=1, source_target_pairs={{0,16},{8,24},{16,0},{24,8},{1,17},{9,25},{17,1},{25,9},{2,18},{10... | collective-permute-start | bytes 8060936 | tf_op jit(solution)/shard_map/ppermute | solution.py:162
  1031.9 94.5 %collective-permute-start.21 = (bf16[2624,256]{1,0:T(8,128)(2,1)}, bf16[2624,256]{1,0:T(8,128)(2,1)}, u32[]{:S(2)}, u32[]{:S(2)}) collective-permute-start(bf16[2624,256]{1,0:T(8,128)(2,1)} %constant_dynamic-slice_fusion.14), channel_id=1, source_target_pairs={{0,16},{8,24},{16,0},{24,8},{1,17},{9,25},{17,1},{25,9},{2,18},{10... | collective-permute-start | bytes 4030472 | tf_op jit(solution)/shard_map/ppermute | solution.py:162
  1035.3 90.9 %collective-permute-start.25 = (bf16[8,32,1024]{2,1,0:T(8,128)(2,1)S(1)}, bf16[8,32,1024]{2,1,0:T(8,128)(2,1)S(1)}, u32[]{:S(2)}, u32[]{:S(2)}) collective-permute-start(bf16[8,32,1024]{2,1,0:T(8,128)(2,1)S(1)} %dynamic-slice_bitcast_fusion.12), channel_id=1, source_target_pairs={{0,16},{8,24},{16,0},{24,8},{1,17},{9,25},{17,1},{25,9},{2,18},{10... | collective-permute-start | bytes 1572872 | tf_op jit(solution)/shard_map/ppermute | solution.py:162
  1147.4 258.0 %reduce-scatter.9.cloned.1.call-start = ((), (), s32[]{:S(2)}) async-start(), calls=%async_computation.9 | async-start | bytes 7004160 | tf_op jit(solution)/shard_map/reduce_scatter | solution.py:236
  1159.2 32.6 %collective-permute-start.17 = (bf16[2624,256]{1,0:T(8,128)(2,1)}, bf16[2624,256]{1,0:T(8,128)(2,1)}, u32[]{:S(2)}, u32[]{:S(2)}) collective-permute-start(bf16[2624,256]{1,0:T(8,128)(2,1)} %constant_dynamic-slice_fusion.16), channel_id=1, source_target_pairs={{0,16},{8,24},{16,0},{24,8},{1,17},{9,25},{17,1},{25,9},{2,18},{10... | collective-permute-start | bytes 4030472 | tf_op jit(solution)/shard_map/ppermute | solution.py:162
  1163.8 60.9 %collective-permute-start.19 = (bf16[8,32,3072]{2,1,0:T(8,128)(2,1)}, bf16[8,32,3072]{2,1,0:T(8,128)(2,1)}, u32[]{:S(2)}, u32[]{:S(2)}) collective-permute-start(bf16[8,32,3072]{2,1,0:T(8,128)(2,1)} %dynamic-slice_bitcast_fusion.8), channel_id=1, source_target_pairs={{0,16},{8,24},{16,0},{24,8},{1,17},{9,25},{17,1},{25,9},{2,18},{10... | collective-permute-start | bytes 4718600 | tf_op jit(solution)/shard_map/ppermute | solution.py:162
  1241.0 231.2 %reduce-scatter.7.cloned.1.call-start = ((), (), s32[]{:S(2)}) async-start(), calls=%async_computation.8 | async-start | bytes 1843200 | tf_op jit(solution)/shard_map/reduce_scatter | solution.py:236
  1290.0 64.7 %collective-permute-start.13 = (bf16[256,2048]{0,1:T(8,128)(2,1)S(1)}, bf16[256,2048]{0,1:T(8,128)(2,1)S(1)}, u32[]{:S(2)}, u32[]{:S(2)}) collective-permute-start(bf16[256,2048]{0,1:T(8,128)(2,1)S(1)} %get-tuple-element.909), channel_id=1, source_target_pairs={{0,1},{1,2},{2,3},{3,4},{4,5},{5,6},{6,7},{8,9},{9,10},{10,11},{11... | collective-permute-start | bytes 3145736 | tf_op jit(solution)/shard_map/ppermute | solution.py:23
  1293.7 61.0 %collective-permute-start.12 = (bf16[256,2048]{0,1:T(8,128)(2,1)S(1)}, bf16[256,2048]{0,1:T(8,128)(2,1)S(1)}, u32[]{:S(2)}, u32[]{:S(2)}) collective-permute-start(bf16[256,2048]{0,1:T(8,128)(2,1)S(1)} %get-tuple-element.908), channel_id=1, source_target_pairs={{1,0},{2,1},{3,2},{4,3},{5,4},{6,5},{7,6},{9,8},{10,9},{11,10},{12... | collective-permute-start | bytes 3145736 | tf_op jit(solution)/shard_map/ppermute | solution.py:23
  1366.3 36.5 %collective-permute-start.15 = (bf16[8,32,3072]{2,1,0:T(8,128)(2,1)S(1)}, bf16[8,32,3072]{2,1,0:T(8,128)(2,1)S(1)}, u32[]{:S(2)}, u32[]{:S(2)}) collective-permute-start(bf16[8,32,3072]{2,1,0:T(8,128)(2,1)S(1)} %dynamic-slice_bitcast_fusion.9), channel_id=1, source_target_pairs={{0,16},{8,24},{16,0},{24,8},{1,17},{9,25},{17,1},{25,9},{2,18},{10... | collective-permute-start | bytes 4718600 | tf_op jit(solution)/shard_map/ppermute | solution.py:162
  1404.8 91.4 %all-gather.33.cloned.1.call-start = ((), (), s32[]{:S(2)}) async-start(), calls=%async_computation.16 | async-start | bytes 2867200 | tf_op jit(solution)/shard_map/all_gather | solution.py:237
  1405.3 120.8 %all-gather.31.cloned.1.call-start = ((), (), s32[]{:S(2)}) async-start(), calls=%async_computation.15 | async-start | bytes 3891200 | tf_op jit(solution)/shard_map/all_gather | solution.py:237
  (145 other events, 2581.1 us)
Sparse Core Ops, SparseCore 0:
  14.1 77.6 all-gather.16
  94.6 127.5 all-gather.22
  225.0 54.4 all-gather.24
  282.1 71.9 all-gather.18
  385.2 123.2 all-gather.20
  511.1 86.1 all-gather.26
  599.4 53.4 all-gather.28
  820.5 147.9 reduce-scatter.4
  1147.5 92.5 reduce-scatter.10
  1243.9 151.8 reduce-scatter.8
  1404.9 67.1 reduce-scatter.6
  1473.5 22.5 all-gather.32
  1497.7 28.3 all-gather.30
